TPU v7x, 256 devices: a whole 4x4x8 slice. The times are simulated.
256 devices in a mesh: row: 16 (over z, x_hi), col: 16 (over y, x_lo, core).
Axes of the slice: x: 4 (x_hi: 2, x_lo: 2; x = x_hi * 2 + x_lo), y: 4, z: 8, core: 2. Of those that a mesh axis runs over, the one named last changes fastest.
Arguments:
- inverse_rows: float32 [1024, 16384], P('row', 'col'), as said below
- tile_mask: int32 [256, 256], replicated, may hold values from 0 to 1, as said below
Outputs:
- covariance: float32 [16384, 16384], P('row', 'col')
Inputs may be any that keep to these rules, and one draw needn't show every extreme that they name: inverse_rows[k, i] is 0 where i > 15360 + k; its magnitudes stay below 8 * 1024**-0.25. tile_mask is 0 above the diagonal and 1 on it.
All inputs are finite; a program needn't handle non-finite values.
Results may differ from a plain program's by a relative error of at most 0.000088.
Values sent between devices are 32-bit elements; how exact they have to be, the bound alone decides.
No kernel may reach another device: no remote copies, remote signals or barrier semaphores. Data moves between devices by JAX's collectives and lax.ppermute only.
A program may use at most 128 MiB of HBM per device.

v0:
```python
import jax
import jax.numpy as jnp
from jax import lax
from jax.sharding import PartitionSpec as P

MT = 64


def occupancy(tile_mask, row_tiles, col_tiles):
    tile_count = tile_mask.shape[0]
    every_tile = jnp.arange(tile_count, dtype=jnp.int32)
    row_pick = (row_tiles[:, None] == every_tile[None, :]).astype(jnp.float32)
    col_pick = (col_tiles[:, None] == every_tile[None, :]).astype(jnp.float32)
    chosen = jnp.dot(
        row_pick,
        tile_mask.astype(jnp.float32),
        precision=lax.Precision.HIGHEST,
        preferred_element_type=jnp.float32,
    )
    return jnp.dot(
        chosen, col_pick.T, precision=lax.Precision.HIGHEST, preferred_element_type=jnp.float32
    )


def masked_products(left_panel, right_panel, wanted):
    rows_local = left_panel.shape[1]
    cols_local = right_panel.shape[1]
    block_rows = min(256, rows_local)
    block_cols = min(256, cols_local)
    count_rows = rows_local // block_rows
    count_cols = cols_local // block_cols
    occupied = (
        wanted.reshape(count_rows, block_rows // MT, count_cols, block_cols // MT).max(axis=(1, 3))
        > 0.5
    )

    def tile_product(entry):
        pair_index, is_used = entry
        first = lax.dynamic_slice_in_dim(
            left_panel, pair_index // count_cols * block_rows, block_rows, 1
        )
        second = lax.dynamic_slice_in_dim(
            right_panel, pair_index % count_cols * block_cols, block_cols, 1
        )

        def compute():
            return lax.dot_general(
                first,
                second,
                (((0,), (0,)), ((), ())),
                precision=lax.Precision.HIGHEST,
                preferred_element_type=jnp.float32,
            )

        def skipped():
            return jnp.zeros((block_rows, block_cols), jnp.float32)

        return lax.cond(is_used, compute, skipped)

    products = lax.map(
        tile_product, (jnp.arange(count_rows * count_cols, dtype=jnp.int32), occupied.reshape(-1))
    )
    local_tiles = (
        products.reshape(count_rows, count_cols, block_rows, block_cols)
        .transpose(0, 2, 1, 3)
        .reshape(rows_local, cols_local)
    )
    tile_rows = rows_local // MT
    tile_cols = cols_local // MT
    expanded = jnp.broadcast_to(wanted[:, None, :, None], (tile_rows, MT, tile_cols, MT)).reshape(
        rows_local, cols_local
    )
    return local_tiles * expanded


def local(inverse_rows, tile_mask):
    row_count = lax.axis_size("row")
    col_count = lax.axis_size("col")
    row_index = lax.axis_index("row")
    col_index = lax.axis_index("col")
    slab_rows, cols_local = inverse_rows.shape
    full_width = cols_local * col_count
    rows_local = full_width // row_count
    right_panel = lax.all_gather(inverse_rows, "row", axis=0, tiled=True)
    whole_rows = lax.all_gather(inverse_rows, "col", axis=1, tiled=True)
    pieces = whole_rows.reshape(slab_rows, row_count, rows_local)
    left_panel = lax.all_to_all(pieces, "row", split_axis=1, concat_axis=0, tiled=True).reshape(
        slab_rows * row_count, rows_local
    )
    row_tiles = row_index * (rows_local // MT) + jnp.arange(rows_local // MT, dtype=jnp.int32)
    col_tiles = col_index * (cols_local // MT) + jnp.arange(cols_local // MT, dtype=jnp.int32)
    wanted = occupancy(tile_mask, row_tiles, col_tiles)
    return masked_products(left_panel, right_panel, wanted)


def solution(mesh):
    return jax.shard_map(
        local,
        mesh=mesh,
        in_specs=(P("row", "col"), P()),
        out_specs=P("row", "col"),
        check_vma=False,
    )
```

profile of v0, /device:TPU:32, one launch (start us, length us, event | category | flops | bytes accessed | tf_op | source)
XLA Modules:
  0.0 368.9 jit_solution(10240504857399059136)
XLA Ops:
  8.0 43.7 %all-gather.3.cloned.1.call-done = f32[64,16384]{1,0:T(8,128)} async-done(((f32[64,1024]{1,0:T(8,128)}), f32[64,16384]{1,0:T(8,128)}) %all-gather.3.cloned.1.call-update) | async-done | bytes 4194320 | tf_op jit(solution)/shard_map/all_gather | solution.py:85
  51.8 4.7 %copy.8 = f32[8,16,8,1024]{3,2,0,1:T(8,128)} copy(f32[8,16,8,1024]{3,2,1,0:T(8,128)} %bitcast.29) | data formatting | bytes 8388608 | tf_op jit(solution)/shard_map/reshape | solution.py:86
  56.5 9.7 %all-to-all-start = ((f32[64,16,1024]{2,0,1:T(8,128)}), f32[64,16,1024]{2,0,1:T(8,128)}, u32[]{:S(2)}, u32[]{:S(2)}) async-start(f32[64,16,1024]{2,0,1:T(8,128)} %bitcast.26), calls=%async_computation | async-start | bytes 8388608 | tf_op jit(solution)/shard_map/all_to_all | solution.py:87
  67.0 3.8 %broadcast_in_dim.27 = f32[16,64,16,64]{3,2,1,0:T(8,128)} broadcast(f32[16,16]{1,0:T(8,128)S(1)} %fusion.5), dimensions={0,2} | broadcast | bytes 4195328 | tf_op jit(solution)/shard_map/broadcast_in_dim | solution.py:70
  70.8 7.6 %reshape.39 = f32[1024,1024]{1,0:T(8,128)} reshape(f32[16,64,16,64]{3,2,1,0:T(8,128)} %broadcast_in_dim.27) | data formatting | bytes 8388608 | tf_op jit(solution)/shard_map/reshape | solution.py:70
  78.4 140.6 %all-gather.5.cloned.1.call-done = f32[1024,1024]{1,0:T(8,128)} async-done(((f32[64,1024]{1,0:T(8,128)}), f32[1024,1024]{1,0:T(8,128)}) %all-gather.5.cloned.1.call-update) | async-done | bytes 4194320 | tf_op jit(solution)/shard_map/all_gather | solution.py:84
  219.1 133.0 %while.12 = (s32[]{:T(128)}, f32[16,256,256]{2,1,0:T(8,128)}, pred[16]{0:T(512)(128)(4,1)S(1)}, s32[16]{0:T(128)S(1)}, f32[1024,1024]{1,0:T(8,128)}, /*index=5*/f32[1024,1024]{1,0:T(8,128)}, s32[]{:T(128)}, s32[]{:T(128)}) while((s32[]{:T(128)}, f32[16,256,256]{2,1,0:T(8,128)}, pred[16]{0:T(512)(128)(4,1)S(1)}, s32[16]{0:T(128)S(1)}, ...), condition=%wide.region_4.5_spmd, body=%wide.region_1.4_spmd.sunk | while | flops 805306368 | bytes 2884547 | solution.py:60
  221.0 5.7 %conditional.2 = (f32[1,256,256]{2,1,0:T(8,128)S(1)}) conditional(s32[]{:T(128)} %bitcast.23, () %tuple.89, (s32[]{:T(128)}, s32[]{:T(128)}, s32[]{:T(128)}, f32[1024,1024]{1,0:T(8,128)}, f32[1024,1024]{1,0:T(8,128)}, /*index=5*/s32[]{:T(128)}) %tuple.90), branch_computations={%region_2.2_spmd, %region_3.3_spmd.clone} | conditional | flops 805306368 | bytes 2359591 | solution.py:58
  229.3 5.7 %conditional.2 = (f32[1,256,256]{2,1,0:T(8,128)S(1)}) conditional(s32[]{:T(128)} %bitcast.23, () %tuple.89, (s32[]{:T(128)}, s32[]{:T(128)}, s32[]{:T(128)}, f32[1024,1024]{1,0:T(8,128)}, f32[1024,1024]{1,0:T(8,128)}, /*index=5*/s32[]{:T(128)}) %tuple.90), branch_computations={%region_2.2_spmd, %region_3.3_spmd.clone} | conditional | flops 805306368 | bytes 2359591 | solution.py:58
  237.6 5.7 %conditional.2 = (f32[1,256,256]{2,1,0:T(8,128)S(1)}) conditional(s32[]{:T(128)} %bitcast.23, () %tuple.89, (s32[]{:T(128)}, s32[]{:T(128)}, s32[]{:T(128)}, f32[1024,1024]{1,0:T(8,128)}, f32[1024,1024]{1,0:T(8,128)}, /*index=5*/s32[]{:T(128)}) %tuple.90), branch_computations={%region_2.2_spmd, %region_3.3_spmd.clone} | conditional | flops 805306368 | bytes 2359591 | solution.py:58
  245.9 5.7 %conditional.2 = (f32[1,256,256]{2,1,0:T(8,128)S(1)}) conditional(s32[]{:T(128)} %bitcast.23, () %tuple.89, (s32[]{:T(128)}, s32[]{:T(128)}, s32[]{:T(128)}, f32[1024,1024]{1,0:T(8,128)}, f32[1024,1024]{1,0:T(8,128)}, /*index=5*/s32[]{:T(128)}) %tuple.90), branch_computations={%region_2.2_spmd, %region_3.3_spmd.clone} | conditional | flops 805306368 | bytes 2359591 | solution.py:58
  254.2 5.7 %conditional.2 = (f32[1,256,256]{2,1,0:T(8,128)S(1)}) conditional(s32[]{:T(128)} %bitcast.23, () %tuple.89, (s32[]{:T(128)}, s32[]{:T(128)}, s32[]{:T(128)}, f32[1024,1024]{1,0:T(8,128)}, f32[1024,1024]{1,0:T(8,128)}, /*index=5*/s32[]{:T(128)}) %tuple.90), branch_computations={%region_2.2_spmd, %region_3.3_spmd.clone} | conditional | flops 805306368 | bytes 2359591 | solution.py:58
  262.5 5.7 %conditional.2 = (f32[1,256,256]{2,1,0:T(8,128)S(1)}) conditional(s32[]{:T(128)} %bitcast.23, () %tuple.89, (s32[]{:T(128)}, s32[]{:T(128)}, s32[]{:T(128)}, f32[1024,1024]{1,0:T(8,128)}, f32[1024,1024]{1,0:T(8,128)}, /*index=5*/s32[]{:T(128)}) %tuple.90), branch_computations={%region_2.2_spmd, %region_3.3_spmd.clone} | conditional | flops 805306368 | bytes 2359591 | solution.py:58
  270.8 5.7 %conditional.2 = (f32[1,256,256]{2,1,0:T(8,128)S(1)}) conditional(s32[]{:T(128)} %bitcast.23, () %tuple.89, (s32[]{:T(128)}, s32[]{:T(128)}, s32[]{:T(128)}, f32[1024,1024]{1,0:T(8,128)}, f32[1024,1024]{1,0:T(8,128)}, /*index=5*/s32[]{:T(128)}) %tuple.90), branch_computations={%region_2.2_spmd, %region_3.3_spmd.clone} | conditional | flops 805306368 | bytes 2359591 | solution.py:58
  279.1 5.7 %conditional.2 = (f32[1,256,256]{2,1,0:T(8,128)S(1)}) conditional(s32[]{:T(128)} %bitcast.23, () %tuple.89, (s32[]{:T(128)}, s32[]{:T(128)}, s32[]{:T(128)}, f32[1024,1024]{1,0:T(8,128)}, f32[1024,1024]{1,0:T(8,128)}, /*index=5*/s32[]{:T(128)}) %tuple.90), branch_computations={%region_2.2_spmd, %region_3.3_spmd.clone} | conditional | flops 805306368 | bytes 2359591 | solution.py:58
  287.5 5.7 %conditional.2 = (f32[1,256,256]{2,1,0:T(8,128)S(1)}) conditional(s32[]{:T(128)} %bitcast.23, () %tuple.89, (s32[]{:T(128)}, s32[]{:T(128)}, s32[]{:T(128)}, f32[1024,1024]{1,0:T(8,128)}, f32[1024,1024]{1,0:T(8,128)}, /*index=5*/s32[]{:T(128)}) %tuple.90), branch_computations={%region_2.2_spmd, %region_3.3_spmd.clone} | conditional | flops 805306368 | bytes 2359591 | solution.py:58
  295.8 5.7 %conditional.2 = (f32[1,256,256]{2,1,0:T(8,128)S(1)}) conditional(s32[]{:T(128)} %bitcast.23, () %tuple.89, (s32[]{:T(128)}, s32[]{:T(128)}, s32[]{:T(128)}, f32[1024,1024]{1,0:T(8,128)}, f32[1024,1024]{1,0:T(8,128)}, /*index=5*/s32[]{:T(128)}) %tuple.90), branch_computations={%region_2.2_spmd, %region_3.3_spmd.clone} | conditional | flops 805306368 | bytes 2359591 | solution.py:58
  304.1 5.7 %conditional.2 = (f32[1,256,256]{2,1,0:T(8,128)S(1)}) conditional(s32[]{:T(128)} %bitcast.23, () %tuple.89, (s32[]{:T(128)}, s32[]{:T(128)}, s32[]{:T(128)}, f32[1024,1024]{1,0:T(8,128)}, f32[1024,1024]{1,0:T(8,128)}, /*index=5*/s32[]{:T(128)}) %tuple.90), branch_computations={%region_2.2_spmd, %region_3.3_spmd.clone} | conditional | flops 805306368 | bytes 2359591 | solution.py:58
  312.4 5.7 %conditional.2 = (f32[1,256,256]{2,1,0:T(8,128)S(1)}) conditional(s32[]{:T(128)} %bitcast.23, () %tuple.89, (s32[]{:T(128)}, s32[]{:T(128)}, s32[]{:T(128)}, f32[1024,1024]{1,0:T(8,128)}, f32[1024,1024]{1,0:T(8,128)}, /*index=5*/s32[]{:T(128)}) %tuple.90), branch_computations={%region_2.2_spmd, %region_3.3_spmd.clone} | conditional | flops 805306368 | bytes 2359591 | solution.py:58
  320.7 5.7 %conditional.2 = (f32[1,256,256]{2,1,0:T(8,128)S(1)}) conditional(s32[]{:T(128)} %bitcast.23, () %tuple.89, (s32[]{:T(128)}, s32[]{:T(128)}, s32[]{:T(128)}, f32[1024,1024]{1,0:T(8,128)}, f32[1024,1024]{1,0:T(8,128)}, /*index=5*/s32[]{:T(128)}) %tuple.90), branch_computations={%region_2.2_spmd, %region_3.3_spmd.clone} | conditional | flops 805306368 | bytes 2359591 | solution.py:58
  329.0 5.7 %conditional.2 = (f32[1,256,256]{2,1,0:T(8,128)S(1)}) conditional(s32[]{:T(128)} %bitcast.23, () %tuple.89, (s32[]{:T(128)}, s32[]{:T(128)}, s32[]{:T(128)}, f32[1024,1024]{1,0:T(8,128)}, f32[1024,1024]{1,0:T(8,128)}, /*index=5*/s32[]{:T(128)}) %tuple.90), branch_computations={%region_2.2_spmd, %region_3.3_spmd.clone} | conditional | flops 805306368 | bytes 2359591 | solution.py:58
  337.3 5.7 %conditional.2 = (f32[1,256,256]{2,1,0:T(8,128)S(1)}) conditional(s32[]{:T(128)} %bitcast.23, () %tuple.89, (s32[]{:T(128)}, s32[]{:T(128)}, s32[]{:T(128)}, f32[1024,1024]{1,0:T(8,128)}, f32[1024,1024]{1,0:T(8,128)}, /*index=5*/s32[]{:T(128)}) %tuple.90), branch_computations={%region_2.2_spmd, %region_3.3_spmd.clone} | conditional | flops 805306368 | bytes 2359591 | solution.py:58
  345.6 5.7 %conditional.2 = (f32[1,256,256]{2,1,0:T(8,128)S(1)}) conditional(s32[]{:T(128)} %bitcast.23, () %tuple.89, (s32[]{:T(128)}, s32[]{:T(128)}, s32[]{:T(128)}, f32[1024,1024]{1,0:T(8,128)}, f32[1024,1024]{1,0:T(8,128)}, /*index=5*/s32[]{:T(128)}) %tuple.90), branch_computations={%region_2.2_spmd, %region_3.3_spmd.clone} | conditional | flops 805306368 | bytes 2359591 | solution.py:58
  352.1 4.9 %copy.4 = f32[4,4,256,256]{3,1,2,0:T(4,128)S(1)} copy(f32[4,4,256,256]{3,2,1,0:T(8,128)} %bitcast.28) | data formatting | bytes 8388608 | tf_op jit(solution)/shard_map/reshape | solution.py:64
  (85 shorter events, 92.1 us)
Async XLA Ops:
  6.5 45.2 %all-gather.3.cloned.1.call-start = ((), (), s32[]{:S(2)}) async-start(), calls=%async_computation.1 | async-start | bytes 4456448 | tf_op jit(solution)/shard_map/all_gather | solution.py:85
  7.3 211.8 %all-gather.5.cloned.1.call-start = ((), (), s32[]{:S(2)}) async-start(), calls=%async_computation.2 | async-start | bytes 4456448 | tf_op jit(solution)/shard_map/all_gather | solution.py:84
  56.5 9.8 %copy-start.1 = (s32[256,256]{1,0:T(8,128)S(1)}, s32[256,256]{1,0:T(8,128)}, u32[]{:S(2)}) copy-start(s32[256,256]{1,0:T(8,128)} %param.7) | copy-start | bytes 786436
  56.5 162.6 %all-to-all-start = ((f32[64,16,1024]{2,0,1:T(8,128)}), f32[64,16,1024]{2,0,1:T(8,128)}, u32[]{:S(2)}, u32[]{:S(2)}) async-start(f32[64,16,1024]{2,0,1:T(8,128)} %bitcast.26), calls=%async_computation | async-start | bytes 8388608 | tf_op jit(solution)/shard_map/all_to_all | solution.py:87
  356.9 2.2 copy-start
Sparse Core Ops, SparseCore 0:
  9.2 42.5 all-gather.2
  54.3 164.6 all-gather.4
where the time goes:
time: 370 us; the launch traced here: 369 us
  waiting for transfers between devices  186 us (50%)
  matrix products  54.4 us (15%)
  local copies, waits for them, and re-layouts  54.2 us (15%)
  loops' own time  48.2 us (13%)
  between operations  13.5 us (4%)
  starting transfers between devices  9.79 us (3%)
    all_gather x1, waiting for transfers between devices, local(): right_panel = lax.all_gather(inverse_rows, 'row', axis=0, tiled=True)  141 us
    dot_general x16, matrix products, compute(): lax.dot_general(first, second, (((0,), (0,)), ((), ())), precision=lax.Pr...  54 us
    all_gather x1, waiting for transfers between devices, local(): whole_rows = lax.all_gather(inverse_rows, 'col', axis=1, tiled=True)  43.7 us
    another operation x16, loops' own time, tile_product(): return lax.cond(is_used, compute, skipped)  37.2 us
    dynamic_slice x32, local copies, waits for them, and re-layouts, masked_products(): lax.map(tile_product, (jnp.arange(count_rows * count_cols, dtype=jnp.int3...  19.2 us
    dynamic_update_slice x16, local copies, waits for them, and re-layouts, masked_products(): lax.map(tile_product, (jnp.arange(count_rows * count_cols, dtype=jnp.int3...  11.6 us
    another operation x1, loops' own time, masked_products(): lax.map(tile_product, (jnp.arange(count_rows * count_cols, dtype=jnp.int3...  11 us
    all_to_all x1, starting transfers between devices, local(): lax.all_to_all(pieces, 'row', split_axis=1, concat_axis=0, tiled=True)  9.75 us
  transfers between devices with their start and end apart: 3, of which 2 were waited for; matrix products, arithmetic and copies ran while one was open for 5% of the time, Pallas kernels for 0%

commit v1 on v0

v1 whole, which is shorter than its diff:
```python
import jax
import jax.numpy as jnp
from jax import lax
from jax.experimental import pallas as pl
from jax.experimental.pallas import tpu as pltpu
from jax.sharding import PartitionSpec as P

MT = 64
AXES = ("row", "col")
NZ = 8
NM = 8
STRIPE = 256


def permute(value, move):
    pairs = []
    for row in range(2 * NZ):
        for col in range(2 * NM):
            xh, m, z, core = move(row % 2, col // 2, row // 2, col % 2)
            pairs.append(
                (row * 2 * NM + col, (z % NZ * 2 + xh) * 2 * NM + m % NM * 2 + core)
            )
    return lax.ppermute(value, AXES, pairs)


def up_z(xh, m, z, core):
    return xh, m, z + 1, core


def down_z(xh, m, z, core):
    return xh, m, z - 1, core


def up_y(xh, m, z, core):
    return xh, m + 2, z, core


def down_y(xh, m, z, core):
    return xh, m - 2, z, core


def other_core(xh, m, z, core):
    return xh, m, z, 1 - core


def ring(block):
    half = block.shape[0] // 2
    p1 = permute(block, up_z)
    m1 = permute(block, down_z)
    p2 = permute(p1, up_z)
    m2 = permute(m1, down_z)
    p3 = permute(p2, up_z)
    m3 = permute(m2, down_z)
    p4 = permute(p3[:half], up_z)
    m4 = permute(m3[half:], down_z)
    return [block, p1, m1, p2, m2, p3, m3, p4, m4]


RING_SHIFT = (0, -1, 1, -2, 2, -3, 3, 4, 4)


def kernel(where, mask_ref, *refs):
    n_right, n_left = 18, 8
    right_in = refs[:n_right]
    left_in = refs[n_right : n_right + n_left]
    out_ref = refs[n_right + n_left]
    left, right, right_hi, right_lo, product, sems, out_sems = refs[n_right + n_left + 1 :]
    z, xh, m, core = where[0], where[1], where[2], where[3]
    active = where[4]
    rows = 64

    copies = []

    def fetch(src, lo, count, buf, slot, offset):
        start = pl.multiple_of(slot * rows + offset, 8)
        copies.append(
            pltpu.make_async_copy(
                src.at[pl.ds(lo, count)], buf.at[pl.ds(start, count)], sems.at[len(copies)]
            )
        )

    def slot_of(zz, x_hi):
        return lax.rem(zz + 2 * NZ, NZ) * 2 + x_hi

    for chain in range(2):
        x_hi = xh if chain == 0 else 1 - xh
        for step in range(9):
            src = right_in[chain * 9 + step]
            slot = slot_of(z + RING_SHIFT[step], x_hi)
            count = src.shape[0]
            fetch(src, 0, count, right, slot, 32 if step == 8 else 0)
    m_other = m + 1 - 2 * lax.rem(m, 2)

    def line_slot(line, kappa):
        return slot_of(lax.rem(line + 2 * NM, NM) - z, kappa)

    pair = (m, m_other)
    layout = [
        (0, 0, pair[0], core), (0, 64, pair[1], core),
        (1, 0, pair[0] - 2, core), (1, 64, pair[1] - 2, core),
        (2, 0, pair[0] + 2, core), (2, 64, pair[1] + 2, core),
        (3, 0, pair[0] + 4, core), (4, 0, pair[1] + 4, core),
        (5, 0, pair[0], 1 - core), (5, 64, pair[1], 1 - core),
        (6, 0, pair[0] - 2, 1 - core), (6, 64, pair[1] - 2, 1 - core),
        (6, 128, pair[0] + 2, 1 - core), (6, 192, pair[1] + 2, 1 - core),
        (7, 0, pair[0] + 4, 1 - core), (7, 64, pair[1] + 4, 1 - core),
    ]
    for array, lo, line, kappa in layout:
        fetch(left_in[array], lo, rows, left, line_slot(line, kappa), 0)
    n_stripes = out_ref.shape[0] // STRIPE

    def store(i):
        return pltpu.make_async_copy(
            product.at[i], out_ref.at[pl.ds(i * STRIPE, STRIPE)], out_sems.at[i]
        )

    @pl.when(active == 0)
    def _():
        for i in range(n_stripes):
            product[i] = jnp.zeros_like(product[i])
            store(i).start()

    @pl.when(active != 0)
    def _():
        for copy in copies:
            copy.start()
        for copy in copies:
            copy.wait()
        full = right[...]
        high = full.astype(jnp.bfloat16)
        right_hi[...] = high
        right_lo[...] = (full - high.astype(jnp.float32)).astype(jnp.bfloat16)
        for i in range(n_stripes):
            part = left[:, i * STRIPE : (i + 1) * STRIPE]
            part_hi = part.astype(jnp.bfloat16)
            part_lo = (part - part_hi.astype(jnp.float32)).astype(jnp.bfloat16)

            def dot(a, b):
                return lax.dot_general(
                    a, b, (((0,), (0,)), ((), ())), preferred_element_type=jnp.float32
                )

            total = (
                dot(part_hi, right_lo[...]) + dot(part_lo, right_hi[...])
            ) + dot(part_hi, right_hi[...])
            for t in range(STRIPE // MT):
                tile = i * (STRIPE // MT) + t
                product[i, t * MT : (t + 1) * MT, :] = (
                    total[t * MT : (t + 1) * MT] * mask_ref[tile : tile + 1, :]
                )
            store(i).start()

    for i in range(n_stripes):
        store(i).wait()


def local(inverse_rows, tile_mask):
    row = lax.axis_index("row")
    col = lax.axis_index("col")
    z, xh = row // 2, row % 2
    m, core = col // 2, col % 2
    cols = inverse_rows.shape[1]
    n_tiles = cols // MT

    spread = permute(inverse_rows, lambda xh, m, z, core: (core, m + z, z, xh))
    mine = permute(spread, lambda xh, m, z, core: (xh, m, m - z, core))
    beside = permute(mine, lambda xh, m, z, core: (xh, m ^ 1, z, core))
    both = jnp.concatenate([mine, beside])
    y1 = permute(both, up_y)
    y3 = permute(both, down_y)
    y2a = permute(y1[:64], up_y)
    y2b = permute(y3[64:], down_y)
    c0 = permute(both, other_core)
    c1 = permute(jnp.concatenate([y1, y3]), other_core)
    c2 = permute(jnp.concatenate([y2a, y2b]), other_core)
    left = [both, y1, y3, y2a, y2b, c0, c1, c2]

    partner = permute(inverse_rows, lambda xh, m, z, core: (1 - xh, m, z, core))
    right = ring(inverse_rows) + ring(partner)

    block = lax.dynamic_slice(tile_mask, (row * n_tiles, col * n_tiles), (n_tiles, n_tiles))
    mask = jnp.broadcast_to(block[:, :, None], (n_tiles, n_tiles, MT)).reshape(n_tiles, cols)
    where = jnp.stack([z, xh, m, core, (row >= col).astype(jnp.int32)]).astype(jnp.int32)
    any_spec = pl.BlockSpec(memory_space=pl.ANY)
    depth = 1024
    return pl.pallas_call(
        kernel,
        out_shape=jax.ShapeDtypeStruct((cols, cols), jnp.float32),
        in_specs=[
            pl.BlockSpec(memory_space=pltpu.SMEM),
            pl.BlockSpec(memory_space=pltpu.VMEM),
        ]
        + [any_spec] * (len(right) + len(left)),
        out_specs=any_spec,
        scratch_shapes=[
            pltpu.VMEM((depth, cols), jnp.float32),
            pltpu.VMEM((depth, cols), jnp.float32),
            pltpu.VMEM((depth, cols), jnp.bfloat16),
            pltpu.VMEM((depth, cols), jnp.bfloat16),
            pltpu.VMEM((cols // STRIPE, STRIPE, cols), jnp.float32),
            pltpu.SemaphoreType.DMA((len(right) + 16,)),
            pltpu.SemaphoreType.DMA((cols // STRIPE,)),
        ],
        compiler_params=pltpu.CompilerParams(vmem_limit_bytes=40 * 1024 * 1024),
    )(where, mask.astype(jnp.float32), *right, *left)


def solution(mesh):
    return jax.shard_map(
        local,
        mesh=mesh,
        in_specs=(P("row", "col"), P()),
        out_specs=P("row", "col"),
        check_vma=False,
    )
```

time: 370 us -> 124 us (0.34)
  the two profiles are of different devices: /device:TPU:32 before, /device:TPU:0 now
where the time goes in v1:
time: 124 us; the launch traced here: 123 us
  starting transfers between devices  63.3 us (51%)
  local copies, waits for them, and re-layouts  23.6 us (19%)
  waiting for transfers between devices  21.9 us (18%)
  Pallas kernels  11 us (9%)
  other arithmetic  2.7 us (2%)
    ppermute x27, starting transfers between devices, permute(): return lax.ppermute(value, AXES, pairs)  63.3 us
    ppermute x27, waiting for transfers between devices, permute(): return lax.ppermute(value, AXES, pairs)  21.9 us
    unnamed x59, local copies, waits for them, and re-layouts  20.4 us
    pallas_call x1, Pallas kernels, local(): pl.pallas_call(kernel, out_shape=jax.ShapeDtypeStruct((cols, cols), jnp.f...  11 us
  transfers between devices with their start and end apart: 27, of which 10 were waited for; matrix products, arithmetic and copies ran while one was open for 5% of the time, Pallas kernels for 0%

profile of v1, /device:TPU:0, one launch (start us, length us, event | category | flops | bytes accessed | tf_op | source)
XLA Modules:
  0.0 123.0 jit_solution(3871631188275992091)
XLA Ops:
  0.0 1.6 %collective-permute-start.17 = (f32[64,1024]{1,0:T(8,128)}, f32[64,1024]{1,0:T(8,128)S(1)}, u32[]{:S(2)}, u32[]{:S(2)}) collective-permute-start(f32[64,1024]{1,0:T(8,128)} %refs_0_.1), channel_id=1, source_target_pairs={{0,0},{1,16},{2,2},{3,18},{4,4},{5,20},{6,6},{7,22},{8,8},{9,24},{... | collective-permute-start | bytes 786440 | tf_op jit(solution)/shard_map/ppermute | solution.py:23
  2.3 22.6 %collective-permute-start.19 = (f32[64,1024]{1,0:T(8,128)S(1)}, f32[64,1024]{1,0:T(8,128)S(1)}, u32[]{:S(2)}, u32[]{:S(2)}) collective-permute-start(f32[64,1024]{1,0:T(8,128)S(1)} %collective-permute-done.18), channel_id=1, source_target_pairs={{0,2},{1,3},{2,0},{3,1},{4,6},{5,7},{6,4},{7,5},{8,10},{9,11},{10,... | collective-permute-start | bytes 786440 | tf_op jit(solution)/shard_map/ppermute | solution.py:23
  25.8 4.8 %collective-permute-start.1 = (f32[64,1024]{1,0:T(8,128)}, f32[64,1024]{1,0:T(8,128)S(1)}, u32[]{:S(2)}, u32[]{:S(2)}) collective-permute-start(f32[64,1024]{1,0:T(8,128)} %refs_0_.1), channel_id=1, source_target_pairs={{0,224},{1,225},{2,226},{3,227},{4,228},{5,229},{6,230},{7,231},{8... | collective-permute-start | bytes 786440 | tf_op jit(solution)/shard_map/ppermute | solution.py:23
  30.7 1.3 %collective-permute-done.19 = f32[64,1024]{1,0:T(8,128)S(1)} collective-permute-done((f32[64,1024]{1,0:T(8,128)S(1)}, f32[64,1024]{1,0:T(8,128)S(1)}, u32[]{:S(2)}, u32[]{:S(2)}) %collective-permute-start.19) | collective-permute-done | bytes 262176 | tf_op jit(solution)/shard_map/ppermute | solution.py:23
  32.0 9.7 %collective-permute-start.21 = (f32[128,1024]{1,0:T(8,128)S(1)}, f32[128,1024]{1,0:T(8,128)S(1)}, u32[]{:S(2)}, u32[]{:S(2)}) collective-permute-start(f32[128,1024]{1,0:T(8,128)S(1)} %constant_dynamic-update-slice_fusion.refs_18_), channel_id=1, source_target_pairs={{0,12},{1,13},{2,14},{3,15},{4,0},{5,1},{6,2},{7,3},{8,4},{9,5},{1... | collective-permute-start | bytes 1572872 | tf_op jit(solution)/shard_map/ppermute | solution.py:23
  42.6 2.4 %collective-permute-start.10 = (f32[64,1024]{1,0:T(8,128)S(1)}, f32[64,1024]{1,0:T(8,128)S(1)}, u32[]{:S(2)}, u32[]{:S(2)}) collective-permute-start(f32[64,1024]{1,0:T(8,128)S(1)} %collective-permute-done.8.refs_9_), channel_id=1, source_target_pairs={{0,224},{1,225},{2,226},{3,227},{4,228},{5,229},{6,230},{7,231},{8... | collective-permute-start | bytes 786440 | tf_op jit(solution)/shard_map/ppermute | solution.py:23
  45.7 6.7 %collective-permute-done.refs_1_ = f32[64,1024]{1,0:T(8,128)S(1)} collective-permute-done((f32[64,1024]{1,0:T(8,128)}, f32[64,1024]{1,0:T(8,128)S(1)}, u32[]{:S(2)}, u32[]{:S(2)}) %collective-permute-start) | collective-permute-done | bytes 262176 | tf_op jit(solution)/shard_map/ppermute | solution.py:23
  52.4 1.9 %collective-permute-start.3 = (f32[64,1024]{1,0:T(8,128)S(1)}, f32[64,1024]{1,0:T(8,128)S(1)}, u32[]{:S(2)}, u32[]{:S(2)}) collective-permute-start(f32[64,1024]{1,0:T(8,128)S(1)} %collective-permute-done.1.refs_2_), channel_id=1, source_target_pairs={{0,224},{1,225},{2,226},{3,227},{4,228},{5,229},{6,230},{7,231},{8... | collective-permute-start | bytes 786440 | tf_op jit(solution)/shard_map/ppermute | solution.py:23
  55.8 2.2 %collective-permute-done.9.refs_10_ = f32[64,1024]{1,0:T(8,128)S(1)} collective-permute-done((f32[64,1024]{1,0:T(8,128)S(1)}, f32[64,1024]{1,0:T(8,128)S(1)}, u32[]{:S(2)}, u32[]{:S(2)}) %collective-permute-start.9) | collective-permute-done | bytes 262176 | tf_op jit(solution)/shard_map/ppermute | solution.py:23
  58.0 1.9 %collective-permute-start.12 = (f32[64,1024]{1,0:T(8,128)S(1)}, f32[64,1024]{1,0:T(8,128)S(1)}, u32[]{:S(2)}, u32[]{:S(2)}) collective-permute-start(f32[64,1024]{1,0:T(8,128)S(1)} %collective-permute-done.10.refs_11_), channel_id=1, source_target_pairs={{0,224},{1,225},{2,226},{3,227},{4,228},{5,229},{6,230},{7,231},{8... | collective-permute-start | bytes 786440 | tf_op jit(solution)/shard_map/ppermute | solution.py:23
  61.4 1.1 pad_maximum_fusion
  62.6 2.4 %collective-permute-start.23 = (f32[64,1024]{1,0:T(8,128)S(1)}, f32[64,1024]{1,0:T(8,128)S(1)}, u32[]{:S(2)}, u32[]{:S(2)}) collective-permute-start(f32[64,1024]{1,0:T(8,128)S(1)} %slice.29), channel_id=1, source_target_pairs={{0,12},{1,13},{2,14},{3,15},{4,0},{5,1},{6,2},{7,3},{8,4},{9,5},{1... | collective-permute-start | bytes 786440 | tf_op jit(solution)/shard_map/ppermute | solution.py:23
  65.0 2.8 %collective-permute-start.5 = (f32[64,1024]{1,0:T(8,128)S(1)}, f32[64,1024]{1,0:T(8,128)S(1)}, u32[]{:S(2)}, u32[]{:S(2)}) collective-permute-start(f32[64,1024]{1,0:T(8,128)S(1)} %collective-permute-done.3.refs_4_), channel_id=1, source_target_pairs={{0,224},{1,225},{2,226},{3,227},{4,228},{5,229},{6,230},{7,231},{8... | collective-permute-start | bytes 786440 | tf_op jit(solution)/shard_map/ppermute | solution.py:23
  68.1 3.2 %collective-permute-done.23.refs_22_ = f32[64,1024]{1,0:T(8,128)S(1)} collective-permute-done((f32[64,1024]{1,0:T(8,128)S(1)}, f32[64,1024]{1,0:T(8,128)S(1)}, u32[]{:S(2)}, u32[]{:S(2)}) %collective-permute-start.23) | collective-permute-done | bytes 262176 | tf_op jit(solution)/shard_map/ppermute | solution.py:23
  71.4 3.1 %collective-permute-start.14 = (f32[64,1024]{1,0:T(8,128)S(1)}, f32[64,1024]{1,0:T(8,128)S(1)}, u32[]{:S(2)}, u32[]{:S(2)}) collective-permute-start(f32[64,1024]{1,0:T(8,128)S(1)} %collective-permute-done.12.refs_13_), channel_id=1, source_target_pairs={{0,224},{1,225},{2,226},{3,227},{4,228},{5,229},{6,230},{7,231},{8... | collective-permute-start | bytes 786440 | tf_op jit(solution)/shard_map/ppermute | solution.py:23
  75.4 1.4 %collective-permute-done.4.refs_5_ = f32[64,1024]{1,0:T(8,128)S(1)} collective-permute-done((f32[64,1024]{1,0:T(8,128)S(1)}, f32[64,1024]{1,0:T(8,128)S(1)}, u32[]{:S(2)}, u32[]{:S(2)}) %collective-permute-start.4) | collective-permute-done | bytes 262176 | tf_op jit(solution)/shard_map/ppermute | solution.py:23
  77.6 2.3 %collective-permute-done.14.refs_15_ = f32[64,1024]{1,0:T(8,128)S(1)} collective-permute-done((f32[64,1024]{1,0:T(8,128)S(1)}, f32[64,1024]{1,0:T(8,128)S(1)}, u32[]{:S(2)}, u32[]{:S(2)}) %collective-permute-start.14) | collective-permute-done | bytes 262176 | tf_op jit(solution)/shard_map/ppermute | solution.py:23
  79.9 3.7 %collective-permute-start.7 = (f32[32,1024]{1,0:T(8,128)S(1)}, f32[32,1024]{1,0:T(8,128)S(1)}, u32[]{:S(2)}, u32[]{:S(2)}) collective-permute-start(f32[32,1024]{1,0:T(8,128)S(1)} %slice.25), channel_id=1, source_target_pairs={{0,224},{1,225},{2,226},{3,227},{4,228},{5,229},{6,230},{7,231},{8... | collective-permute-start | bytes 393224 | tf_op jit(solution)/shard_map/ppermute | solution.py:23
  86.8 3.7 %collective-permute-start.16 = (f32[32,1024]{1,0:T(8,128)}, f32[32,1024]{1,0:T(8,128)}, u32[]{:S(2)}, u32[]{:S(2)}) collective-permute-start(f32[32,1024]{1,0:T(8,128)} %slice.27), channel_id=1, source_target_pairs={{0,224},{1,225},{2,226},{3,227},{4,228},{5,229},{6,230},{7,231},{8... | collective-permute-start | bytes 393224 | tf_op jit(solution)/shard_map/ppermute | solution.py:23
  92.6 1.0 convert_element_type.7.mask_ref
  93.7 3.9 %collective-permute-done.15.refs_16_ = f32[32,1024]{1,0:T(8,128)} collective-permute-done((f32[32,1024]{1,0:T(8,128)}, f32[32,1024]{1,0:T(8,128)}, u32[]{:S(2)}, u32[]{:S(2)}) %collective-permute-start.15) | collective-permute-done | bytes 131104 | tf_op jit(solution)/shard_map/ppermute | solution.py:23
  99.5 0.9 copy-done.5
  100.5 0.9 copy-done.6
  111.8 11.0 %shard_map.28 = f32[1024,1024]{1,0:T(8,128)} custom-call(s32[5]{0:T(128)S(1)} %stack.27.where, f32[16,1024]{1,0:T(8,128)S(1)} %convert_element_type.7.mask_ref, f32[64,1024]{1,0:T(8,128)S(1)} %copy-done.6, f32[64,1024]{1,0:T(8,128)S(1)} %copy-done.12, f32[64,1024]{1,0:T(8,128)S(1)} %copy-done.10, f32[64,1024]{1,0:T(8,128)S(1)} %copy-done.20, ...), custom_call_target="tpu_custom_call" | custom-call | tf_op jit(solution)/shard_map/pallas_call | solution.py:186
  (103 shorter events, 26.2 us)
Async XLA Ops:
  2.3 29.7 %collective-permute-start.19 = (f32[64,1024]{1,0:T(8,128)S(1)}, f32[64,1024]{1,0:T(8,128)S(1)}, u32[]{:S(2)}, u32[]{:S(2)}) collective-permute-start(f32[64,1024]{1,0:T(8,128)S(1)} %collective-permute-done.18), channel_id=1, source_target_pairs={{0,2},{1,3},{2,0},{3,1},{4,6},{5,7},{6,4},{7,5},{8,10},{9,11},{10,... | collective-permute-start | bytes 786440 | tf_op jit(solution)/shard_map/ppermute | solution.py:23
  24.9 17.7 %collective-permute-start.8 = (f32[64,1024]{1,0:T(8,128)}, f32[64,1024]{1,0:T(8,128)S(1)}, u32[]{:S(2)}, u32[]{:S(2)}) collective-permute-start(f32[64,1024]{1,0:T(8,128)} %refs_0_.1), channel_id=1, source_target_pairs={{0,16},{1,17},{2,18},{3,19},{4,20},{5,21},{6,22},{7,23},{8,24},{9,... | collective-permute-start | bytes 786440 | tf_op jit(solution)/shard_map/ppermute | solution.py:23
  25.8 19.2 %collective-permute-start.1 = (f32[64,1024]{1,0:T(8,128)}, f32[64,1024]{1,0:T(8,128)S(1)}, u32[]{:S(2)}, u32[]{:S(2)}) collective-permute-start(f32[64,1024]{1,0:T(8,128)} %refs_0_.1), channel_id=1, source_target_pairs={{0,224},{1,225},{2,226},{3,227},{4,228},{5,229},{6,230},{7,231},{8... | collective-permute-start | bytes 786440 | tf_op jit(solution)/shard_map/ppermute | solution.py:23
  32.0 28.5 %collective-permute-start.21 = (f32[128,1024]{1,0:T(8,128)S(1)}, f32[128,1024]{1,0:T(8,128)S(1)}, u32[]{:S(2)}, u32[]{:S(2)}) collective-permute-start(f32[128,1024]{1,0:T(8,128)S(1)} %constant_dynamic-update-slice_fusion.refs_18_), channel_id=1, source_target_pairs={{0,12},{1,13},{2,14},{3,15},{4,0},{5,1},{6,2},{7,3},{8,4},{9,5},{1... | collective-permute-start | bytes 1572872 | tf_op jit(solution)/shard_map/ppermute | solution.py:23
  41.7 19.7 %collective-permute-start.20 = (f32[128,1024]{1,0:T(8,128)S(1)}, f32[128,1024]{1,0:T(8,128)S(1)}, u32[]{:S(2)}, u32[]{:S(2)}) collective-permute-start(f32[128,1024]{1,0:T(8,128)S(1)} %constant_dynamic-update-slice_fusion.refs_18_), channel_id=1, source_target_pairs={{0,4},{1,5},{2,6},{3,7},{4,8},{5,9},{6,10},{7,11},{8,12},{9,13},{1... | collective-permute-start | bytes 1572872 | tf_op jit(solution)/shard_map/ppermute | solution.py:23
  41.7 10.7 %collective-permute-start = (f32[64,1024]{1,0:T(8,128)}, f32[64,1024]{1,0:T(8,128)S(1)}, u32[]{:S(2)}, u32[]{:S(2)}) collective-permute-start(f32[64,1024]{1,0:T(8,128)} %refs_0_.1), channel_id=1, source_target_pairs={{0,32},{1,33},{2,34},{3,35},{4,36},{5,37},{6,38},{7,39},{8,40},{9,... | collective-permute-start | bytes 786440 | tf_op jit(solution)/shard_map/ppermute | solution.py:23
  42.6 12.4 %collective-permute-start.10 = (f32[64,1024]{1,0:T(8,128)S(1)}, f32[64,1024]{1,0:T(8,128)S(1)}, u32[]{:S(2)}, u32[]{:S(2)}) collective-permute-start(f32[64,1024]{1,0:T(8,128)S(1)} %collective-permute-done.8.refs_9_), channel_id=1, source_target_pairs={{0,224},{1,225},{2,226},{3,227},{4,228},{5,229},{6,230},{7,231},{8... | collective-permute-start | bytes 786440 | tf_op jit(solution)/shard_map/ppermute | solution.py:23
  45.0 13.0 %collective-permute-start.9 = (f32[64,1024]{1,0:T(8,128)S(1)}, f32[64,1024]{1,0:T(8,128)S(1)}, u32[]{:S(2)}, u32[]{:S(2)}) collective-permute-start(f32[64,1024]{1,0:T(8,128)S(1)} %collective-permute-done.8.refs_9_), channel_id=1, source_target_pairs={{0,32},{1,33},{2,34},{3,35},{4,36},{5,37},{6,38},{7,39},{8,40},{9,... | collective-permute-start | bytes 786440 | tf_op jit(solution)/shard_map/ppermute | solution.py:23
  52.4 10.2 %collective-permute-start.3 = (f32[64,1024]{1,0:T(8,128)S(1)}, f32[64,1024]{1,0:T(8,128)S(1)}, u32[]{:S(2)}, u32[]{:S(2)}) collective-permute-start(f32[64,1024]{1,0:T(8,128)S(1)} %collective-permute-done.1.refs_2_), channel_id=1, source_target_pairs={{0,224},{1,225},{2,226},{3,227},{4,228},{5,229},{6,230},{7,231},{8... | collective-permute-start | bytes 786440 | tf_op jit(solution)/shard_map/ppermute | solution.py:23
  55.0 10.0 %collective-permute-start.2 = (f32[64,1024]{1,0:T(8,128)S(1)}, f32[64,1024]{1,0:T(8,128)S(1)}, u32[]{:S(2)}, u32[]{:S(2)}) collective-permute-start(f32[64,1024]{1,0:T(8,128)S(1)} %collective-permute-done.refs_1_), channel_id=1, source_target_pairs={{0,32},{1,33},{2,34},{3,35},{4,36},{5,37},{6,38},{7,39},{8,40},{9,... | collective-permute-start | bytes 786440 | tf_op jit(solution)/shard_map/ppermute | solution.py:23
  58.0 6.9 %collective-permute-start.12 = (f32[64,1024]{1,0:T(8,128)S(1)}, f32[64,1024]{1,0:T(8,128)S(1)}, u32[]{:S(2)}, u32[]{:S(2)}) collective-permute-start(f32[64,1024]{1,0:T(8,128)S(1)} %collective-permute-done.10.refs_11_), channel_id=1, source_target_pairs={{0,224},{1,225},{2,226},{3,227},{4,228},{5,229},{6,230},{7,231},{8... | collective-permute-start | bytes 786440 | tf_op jit(solution)/shard_map/ppermute | solution.py:23
  60.6 7.6 %collective-permute-start.11 = (f32[64,1024]{1,0:T(8,128)S(1)}, f32[64,1024]{1,0:T(8,128)S(1)}, u32[]{:S(2)}, u32[]{:S(2)}) collective-permute-start(f32[64,1024]{1,0:T(8,128)S(1)} %collective-permute-done.9.refs_10_), channel_id=1, source_target_pairs={{0,32},{1,33},{2,34},{3,35},{4,36},{5,37},{6,38},{7,39},{8,40},{9,... | collective-permute-start | bytes 786440 | tf_op jit(solution)/shard_map/ppermute | solution.py:23
  62.5 35.1 %collective-permute-start.25 = (f32[256,1024]{1,0:T(8,128)}, f32[256,1024]{1,0:T(8,128)S(1)}, u32[]{:S(2)}, u32[]{:S(2)}) collective-permute-start(f32[256,1024]{1,0:T(8,128)} %pad_maximum_fusion), channel_id=1, source_target_pairs={{0,1},{1,0},{2,3},{3,2},{4,5},{5,4},{6,7},{7,6},{8,9},{9,8},{10,11... | collective-permute-start | bytes 3145736 | tf_op jit(solution)/shard_map/ppermute | solution.py:23
  62.6 8.8 %collective-permute-start.23 = (f32[64,1024]{1,0:T(8,128)S(1)}, f32[64,1024]{1,0:T(8,128)S(1)}, u32[]{:S(2)}, u32[]{:S(2)}) collective-permute-start(f32[64,1024]{1,0:T(8,128)S(1)} %slice.29), channel_id=1, source_target_pairs={{0,12},{1,13},{2,14},{3,15},{4,0},{5,1},{6,2},{7,3},{8,4},{9,5},{1... | collective-permute-start | bytes 786440 | tf_op jit(solution)/shard_map/ppermute | solution.py:23
  64.9 9.6 %collective-permute-start.22 = (f32[64,1024]{1,0:T(8,128)S(1)}, f32[64,1024]{1,0:T(8,128)S(1)}, u32[]{:S(2)}, u32[]{:S(2)}) collective-permute-start(f32[64,1024]{1,0:T(8,128)S(1)} %slice.28), channel_id=1, source_target_pairs={{0,4},{1,5},{2,6},{3,7},{4,8},{5,9},{6,10},{7,11},{8,12},{9,13},{1... | collective-permute-start | bytes 786440 | tf_op jit(solution)/shard_map/ppermute | solution.py:23
  65.0 10.5 %collective-permute-start.5 = (f32[64,1024]{1,0:T(8,128)S(1)}, f32[64,1024]{1,0:T(8,128)S(1)}, u32[]{:S(2)}, u32[]{:S(2)}) collective-permute-start(f32[64,1024]{1,0:T(8,128)S(1)} %collective-permute-done.3.refs_4_), channel_id=1, source_target_pairs={{0,224},{1,225},{2,226},{3,227},{4,228},{5,229},{6,230},{7,231},{8... | collective-permute-start | bytes 786440 | tf_op jit(solution)/shard_map/ppermute | solution.py:23
  68.1 8.7 %collective-permute-start.4 = (f32[64,1024]{1,0:T(8,128)S(1)}, f32[64,1024]{1,0:T(8,128)S(1)}, u32[]{:S(2)}, u32[]{:S(2)}) collective-permute-start(f32[64,1024]{1,0:T(8,128)S(1)} %collective-permute-done.2.refs_3_), channel_id=1, source_target_pairs={{0,32},{1,33},{2,34},{3,35},{4,36},{5,37},{6,38},{7,39},{8,40},{9,... | collective-permute-start | bytes 786440 | tf_op jit(solution)/shard_map/ppermute | solution.py:23
  71.4 8.5 %collective-permute-start.14 = (f32[64,1024]{1,0:T(8,128)S(1)}, f32[64,1024]{1,0:T(8,128)S(1)}, u32[]{:S(2)}, u32[]{:S(2)}) collective-permute-start(f32[64,1024]{1,0:T(8,128)S(1)} %collective-permute-done.12.refs_13_), channel_id=1, source_target_pairs={{0,224},{1,225},{2,226},{3,227},{4,228},{5,229},{6,230},{7,231},{8... | collective-permute-start | bytes 786440 | tf_op jit(solution)/shard_map/ppermute | solution.py:23
  74.6 9.0 %collective-permute-start.13 = (f32[64,1024]{1,0:T(8,128)S(1)}, f32[64,1024]{1,0:T(8,128)S(1)}, u32[]{:S(2)}, u32[]{:S(2)}) collective-permute-start(f32[64,1024]{1,0:T(8,128)S(1)} %collective-permute-done.11.refs_12_), channel_id=1, source_target_pairs={{0,32},{1,33},{2,34},{3,35},{4,36},{5,37},{6,38},{7,39},{8,40},{9,... | collective-permute-start | bytes 786440 | tf_op jit(solution)/shard_map/ppermute | solution.py:23
  75.4 22.2 %collective-permute-start.24 = (f32[128,1024]{1,0:T(8,128)S(1)}, f32[128,1024]{1,0:T(8,128)}, u32[]{:S(2)}, u32[]{:S(2)}) collective-permute-start(f32[128,1024]{1,0:T(8,128)S(1)} %constant_dynamic-update-slice_fusion.refs_18_), channel_id=1, source_target_pairs={{0,1},{1,0},{2,3},{3,2},{4,5},{5,4},{6,7},{7,6},{8,9},{9,8},{10,11... | collective-permute-start | bytes 1572872 | tf_op jit(solution)/shard_map/ppermute | solution.py:23
  76.9 20.7 %collective-permute-start.26 = (f32[128,1024]{1,0:T(8,128)}, f32[128,1024]{1,0:T(8,128)}, u32[]{:S(2)}, u32[]{:S(2)}) collective-permute-start(f32[128,1024]{1,0:T(8,128)} %pad_maximum_fusion.1), channel_id=1, source_target_pairs={{0,1},{1,0},{2,3},{3,2},{4,5},{5,4},{6,7},{7,6},{8,9},{9,8},{10,11... | collective-permute-start | bytes 1572872 | tf_op jit(solution)/shard_map/ppermute | solution.py:23
  83.6 6.8 %collective-permute-start.6 = (f32[32,1024]{1,0:T(8,128)S(1)}, f32[32,1024]{1,0:T(8,128)S(1)}, u32[]{:S(2)}, u32[]{:S(2)}) collective-permute-start(f32[32,1024]{1,0:T(8,128)S(1)} %slice.24), channel_id=1, source_target_pairs={{0,32},{1,33},{2,34},{3,35},{4,36},{5,37},{6,38},{7,39},{8,40},{9,... | collective-permute-start | bytes 393224 | tf_op jit(solution)/shard_map/ppermute | solution.py:23
  86.8 7.0 %collective-permute-start.16 = (f32[32,1024]{1,0:T(8,128)}, f32[32,1024]{1,0:T(8,128)}, u32[]{:S(2)}, u32[]{:S(2)}) collective-permute-start(f32[32,1024]{1,0:T(8,128)} %slice.27), channel_id=1, source_target_pairs={{0,224},{1,225},{2,226},{3,227},{4,228},{5,229},{6,230},{7,231},{8... | collective-permute-start | bytes 393224 | tf_op jit(solution)/shard_map/ppermute | solution.py:23
  91.1 6.5 %collective-permute-start.15 = (f32[32,1024]{1,0:T(8,128)}, f32[32,1024]{1,0:T(8,128)}, u32[]{:S(2)}, u32[]{:S(2)}) collective-permute-start(f32[32,1024]{1,0:T(8,128)} %slice.26), channel_id=1, source_target_pairs={{0,32},{1,33},{2,34},{3,35},{4,36},{5,37},{6,38},{7,39},{8,40},{9,... | collective-permute-start | bytes 393224 | tf_op jit(solution)/shard_map/ppermute | solution.py:23
  (32 other events, 121.7 us)

commit v2 on v1

v2 whole, which is shorter than its diff:
```python
import functools

import jax
import jax.numpy as jnp
from jax import lax
from jax.experimental import pallas as pl
from jax.experimental.pallas import tpu as pltpu
from jax.sharding import PartitionSpec as P

MT = 64
AXES = ("row", "col")
NZ = 8
NM = 8
STRIPE = 256
WINDOW = 4


def permute(value, move):
    pairs = []
    for row in range(2 * NZ):
        for col in range(2 * NM):
            xh, m, z, core = move(row % 2, col // 2, row // 2, col % 2)
            pairs.append(
                (row * 2 * NM + col, (z % NZ * 2 + xh) * 2 * NM + m % NM * 2 + core)
            )
    return lax.ppermute(value, AXES, pairs)


def along_z(value):
    return permute(value, lambda xh, m, z, core: (xh, m, z + 1 - 2 * core, core))


def along_z_across(value):
    return permute(value, lambda xh, m, z, core: (1 - xh, m, z + 1 - 2 * core, core))


def along_y(value):
    return permute(value, lambda xh, m, z, core: (xh, m + 2 - 4 * core, z, core))


def into_plane(value):
    return permute(value, lambda xh, m, z, core: (core, m + z + 4 * xh, z, xh))


def to_rows(value):
    return permute(value, lambda xh, m, z, core: (xh, m, m - z + 4 * core, core))


def other_core(value):
    return permute(value, lambda xh, m, z, core: (xh, m, z, 1 - core))


def other_xh(value):
    return permute(value, lambda xh, m, z, core: (1 - xh, m, z, core))


def other_xl(value):
    return permute(value, lambda xh, m, z, core: (xh, m ^ 1, z, core))


class Steps:
    def __init__(self, window):
        self.window = window
        self.results = []

    def __call__(self, move, value):
        if len(self.results) >= self.window:
            value, _ = lax.optimization_barrier((value, self.results[-self.window]))
        self.results.append(move(value))
        return self.results[-1]


def after(value, *others):
    return lax.optimization_barrier((value, *others))[0]


class Pieces:
    def __init__(self):
        self.arrays = []
        self.moves = []

    def add(self, array, *moves):
        index = len(self.arrays)
        self.arrays.append(array)
        self.moves += [(index, *move) for move in moves]


def kernel(moves, n_in, where, mask_in, *refs):
    ins = refs[:n_in]
    out_ref = refs[n_in]
    left, right, left_hi, left_lo, right_hi, right_lo, product, mask, mask_rows, sems, mask_sem, out_sems = refs[
        n_in + 1 :
    ]
    z, xh, m, core = where[0], where[1], where[2], where[3]
    row = z * 2 + xh
    col = m * 2 + core
    sign = 1 - 2 * core
    cols = right_hi.shape[1]
    n_tiles = cols // MT
    all_tiles = mask_in.shape[0]

    def right_slot(key):
        steps, flip = key
        zz = lax.rem(z - sign * steps + 2 * NZ, NZ)
        return zz * 2 + (1 - xh if flip else xh)

    def left_slot(key):
        line, swap = key
        kappa = 1 - core if swap else core
        return lax.rem(line - z + 4 * kappa + NZ, NZ) * 2 + kappa

    copies = {"right": [], "left": []}
    for panel, index, first, count, key, offset in moves:
        buf, slot = (right, right_slot(key)) if panel == "right" else (left, left_slot(key))
        start = pl.multiple_of(slot * 64 + offset, 8)
        total = len(copies["right"]) + len(copies["left"])
        copies[panel].append(
            pltpu.make_async_copy(
                ins[index].at[pl.ds(first, count)], buf.at[pl.ds(start, count)], sems.at[total]
            )
        )
    n_stripes = out_ref.shape[0] // STRIPE

    def store(i):
        return pltpu.make_async_copy(
            product.at[i], out_ref.at[pl.ds(i * STRIPE, STRIPE)], out_sems.at[i]
        )

    @pl.when(row < col)
    def _():
        for i in range(n_stripes):
            product[i] = jnp.zeros_like(product[i])
            store(i).start()

    mask_copy = pltpu.make_async_copy(
        mask_in.at[pl.ds(pl.multiple_of(row * n_tiles, 8), n_tiles)], mask_rows, mask_sem
    )

    @pl.when(row >= col)
    def _():
        mask_copy.start()
        for copy in copies["right"] + copies["left"]:
            copy.start()
        tile = lax.broadcasted_iota(jnp.int32, (all_tiles, cols), 0)
        wanted = col * n_tiles + lax.broadcasted_iota(jnp.int32, (all_tiles, cols), 1) // MT
        pick = (tile == wanted).astype(jnp.bfloat16)
        mask_copy.wait()
        mask[...] = jnp.dot(
            mask_rows[...].astype(jnp.float32).astype(jnp.bfloat16),
            pick,
            preferred_element_type=jnp.float32,
        )

        for panel, full, high, low in (
            ("right", right, right_hi, right_lo),
            ("left", left, left_hi, left_lo),
        ):
            for copy in copies[panel]:
                copy.wait()
            rounded = full[...].astype(jnp.bfloat16)
            high[...] = rounded
            low[...] = (full[...] - rounded.astype(jnp.float32)).astype(jnp.bfloat16)

        def dot(a, b):
            return lax.dot_general(
                a, b, (((0,), (0,)), ((), ())), preferred_element_type=jnp.float32
            )

        for i in range(n_stripes):
            part = slice(i * STRIPE, (i + 1) * STRIPE)
            total = (
                dot(left_hi[:, part], right_lo[...]) + dot(left_lo[:, part], right_hi[...])
            ) + dot(left_hi[:, part], right_hi[...])
            for t in range(STRIPE // MT):
                tile = i * (STRIPE // MT) + t
                product[i, t * MT : (t + 1) * MT, :] = (
                    total[t * MT : (t + 1) * MT] * mask[tile : tile + 1, :]
                )
            store(i).start()

    for i in range(n_stripes):
        store(i).wait()


def local(inverse_rows, tile_mask):
    row = lax.axis_index("row")
    col = lax.axis_index("col")
    z, xh = row // 2, row % 2
    m, core = col // 2, col % 2
    cols = inverse_rows.shape[1]
    n = inverse_rows.shape[0]
    depth = n * 2 * NZ
    cat = lambda *parts: jnp.concatenate(parts)

    own = inverse_rows
    spread = into_plane(own)
    own_pair = cat(own, other_core(after(own, own)))
    a1 = along_z(own_pair)
    partner = other_xh(after(own, own))
    mine = to_rows(spread)
    a2 = along_z(after(a1, a1))
    b1 = other_xh(after(a1, a1))
    copies = jnp.broadcast_to(after(mine, mine)[None], (NM, n, cols))
    groups = [[2 * line + k for line in range(NM)] for k in range(2)]
    lines = lax.all_to_all(
        copies, "col", split_axis=0, concat_axis=0, tiled=True, axis_index_groups=groups
    ).reshape(NM * n, cols)
    a1x = other_core(a1)
    b1x = other_core(b1)
    b2 = along_z(after(b1, a2, a1x))
    a3 = along_z(after(a2, a2))
    a2x = other_core(a2)
    b2x = other_core(b2)
    a4 = along_z(after(a3, b2, a2x, b1x)[:n])
    b3 = along_z(after(b2, a3, b2x))
    b4 = along_z(after(b3, a4)[:n])
    a3x = other_core(a3)
    b3x = other_core(b3)
    swapped_lines = other_core(after(lines, a4, b3, partner))
    right = Pieces()
    right.add(own, (0, n, (0, 0), 0))
    right.add(partner, (0, n, (0, 1), 0))
    for steps, a, b, ax, bx in ((1, a1, b1, a1x, b1x), (2, a2, b2, a2x, b2x), (3, a3, b3, a3x, b3x)):
        right.add(a, (0, n, (steps, 0), 0))
        right.add(b, (0, n, (steps, 1), 0))
        right.add(ax, (n, n, (-steps, 0), 0))
        right.add(bx, (n, n, (-steps, 1), 0))
    right.add(a4, (0, n, (4, 0), 0))
    right.add(b4, (0, n, (4, 1), 0))

    left = Pieces()
    left.add(lines, *[(line * n, n, (line, 0), 0) for line in range(NM)])
    left.add(swapped_lines, *[(line * n, n, (line, 1), 0) for line in range(NM)])

    moves = [("right", *move) for move in right.moves]
    moves += [("left", move[0] + len(right.arrays), *move[1:]) for move in left.moves]
    arrays = [
        pltpu.with_memory_space_constraint(a, pltpu.HBM) for a in right.arrays + left.arrays
    ]
    where = jnp.stack([z, xh, m, core]).astype(jnp.int32)
    return pl.pallas_call(
        functools.partial(kernel, moves, len(arrays)),
        out_shape=jax.ShapeDtypeStruct((cols, cols), jnp.float32),
        in_specs=[
            pl.BlockSpec(memory_space=pltpu.SMEM),
            pl.BlockSpec(memory_space=pltpu.HBM),
        ]
        + [pl.BlockSpec(memory_space=pltpu.HBM)] * len(arrays),
        out_specs=pl.BlockSpec(memory_space=pltpu.HBM),
        scratch_shapes=[
            pltpu.VMEM((depth, cols), jnp.float32),
            pltpu.VMEM((depth, cols), jnp.float32),
            pltpu.VMEM((depth, cols), jnp.bfloat16),
            pltpu.VMEM((depth, cols), jnp.bfloat16),
            pltpu.VMEM((depth, cols), jnp.bfloat16),
            pltpu.VMEM((depth, cols), jnp.bfloat16),
            pltpu.VMEM((cols // STRIPE, STRIPE, cols), jnp.float32),
            pltpu.VMEM((cols // MT, cols), jnp.float32),
            pltpu.VMEM((cols // MT, tile_mask.shape[1]), jnp.int32),
            pltpu.SemaphoreType.DMA((len(moves),)),
            pltpu.SemaphoreType.DMA,
            pltpu.SemaphoreType.DMA((cols // STRIPE,)),
        ],
        compiler_params=pltpu.CompilerParams(vmem_limit_bytes=32 * 1024 * 1024),
    )(where, pltpu.with_memory_space_constraint(tile_mask, pltpu.HBM), *arrays)


def solution(mesh):
    return jax.shard_map(
        local,
        mesh=mesh,
        in_specs=(P("row", "col"), P()),
        out_specs=P("row", "col"),
        check_vma=False,
    )
```

time: 124 us -> 96 us (0.77)
  starting transfers between devices: 63.3 us -> 30.5 us
  waiting for transfers between devices: 21.9 us -> 45.6 us
  local copies, waits for them, and re-layouts: 23.6 us -> 5.2 us
  Pallas kernels: 11 us -> 12.7 us
  other arithmetic: 2.7 us -> 1.07 us
    ppermute x27 -> x19, starting transfers between devices: 63.3 us -> 8.99 us  [permute(): return lax.ppermute(value, AXES, pairs)]
    ppermute x27 -> x19, waiting for transfers between devices: 21.9 us -> 45.6 us  [permute(): return lax.ppermute(value, AXES, pairs)]
    all_to_all x0 -> x1, starting transfers between devices: none -> 21.5 us  [local(): lax.all_to_all(copies, 'col', split_axis=0, concat_axis=0, tiled=True, ax...]
    unnamed x59 -> x20, local copies, waits for them, and re-layouts: 20.4 us -> 2.76 us
    pallas_call x1, Pallas kernels: 11 us -> 12.7 us  [local(): pl.pallas_call(functools.partial(kernel, moves, len(arrays)), out_shape=j...]
  transfers between devices with their start and end apart: 27 -> 20, of which waited for: 10 -> 8; matrix products, arithmetic and copies ran while one was open for 5% -> 3% of each run, Pallas kernels for 0% -> 0%
where the time goes in v2:
time: 96 us; the launch traced here: 95.4 us
  waiting for transfers between devices  45.6 us (48%)
  starting transfers between devices  30.5 us (32%)
  Pallas kernels  12.7 us (13%)
  local copies, waits for them, and re-layouts  5.2 us (5%)
  other arithmetic  1.07 us (1%)
    ppermute x19, waiting for transfers between devices, permute(): return lax.ppermute(value, AXES, pairs)  45.6 us
    all_to_all x1, starting transfers between devices, local(): lax.all_to_all(copies, 'col', split_axis=0, concat_axis=0, tiled=True, ax...  21.5 us
    pallas_call x1, Pallas kernels, local(): pl.pallas_call(functools.partial(kernel, moves, len(arrays)), out_shape=j...  12.7 us
    ppermute x19, starting transfers between devices, permute(): return lax.ppermute(value, AXES, pairs)  8.99 us
    unnamed x20, local copies, waits for them, and re-layouts  2.76 us
  transfers between devices with their start and end apart: 20, of which 8 were waited for; matrix products, arithmetic and copies ran while one was open for 3% of the time, Pallas kernels for 0%

profile of v2, /device:TPU:0, one launch (start us, length us, event | category | flops | bytes accessed | tf_op | source)
XLA Modules:
  0.0 95.4 jit_solution(10376785374591269587)
XLA Ops:
  0.0 1.7 %collective-permute-done.1 = f32[64,1024]{1,0:T(8,128)S(1)} collective-permute-done((f32[64,1024]{1,0:T(8,128)}, f32[64,1024]{1,0:T(8,128)S(1)}, u32[]{:S(2)}, u32[]{:S(2)}) %collective-permute-start.1) | collective-permute-done | bytes 262176 | tf_op jit(solution)/shard_map/ppermute | solution.py:26
  1.7 1.0 %pad_maximum_fusion = f32[128,1024]{1,0:T(8,128)S(1)} fusion(f32[64,1024]{1,0:T(8,128)S(1)} %collective-permute-done.1, f32[64,1024]{1,0:T(8,128)} %refs_0_.1), kind=kLoop, calls=%fused_computation | loop fusion | flops 131072 | bytes 1048576 | tf_op jit(solution)/shard_map/concatenate | solution.py:193
  2.7 0.3 collective-permute-start.2
  3.0 1.6 %collective-permute-start.16 = (f32[64,1024]{1,0:T(8,128)}, f32[64,1024]{1,0:T(8,128)S(1)}, u32[]{:S(2)}, u32[]{:S(2)}) collective-permute-start(f32[64,1024]{1,0:T(8,128)} %refs_0_.1), channel_id=1, source_target_pairs={{0,0},{1,16},{2,2},{3,18},{4,4},{5,20},{6,6},{7,22},{8,8},{9,24},{... | collective-permute-start | bytes 786440 | tf_op jit(solution)/shard_map/ppermute | solution.py:26
  4.6 9.5 %collective-permute-done.2.refs_2_ = f32[128,1024]{1,0:T(8,128)S(1)} collective-permute-done((f32[128,1024]{1,0:T(8,128)S(1)}, f32[128,1024]{1,0:T(8,128)S(1)}, u32[]{:S(2)}, u32[]{:S(2)}) %collective-permute-start.2) | collective-permute-done | bytes 524320 | tf_op jit(solution)/shard_map/ppermute | solution.py:26
  14.1 3.0 %collective-permute-start.3 = (f32[128,1024]{1,0:T(8,128)S(1)}, f32[128,1024]{1,0:T(8,128)}, u32[]{:S(2)}, u32[]{:S(2)}) collective-permute-start(f32[128,1024]{1,0:T(8,128)S(1)} %collective-permute-done.2.refs_2_), channel_id=1, source_target_pairs={{0,16},{1,17},{2,18},{3,19},{4,20},{5,21},{6,22},{7,23},{8,24},{9,... | collective-permute-start | bytes 1572872 | tf_op jit(solution)/shard_map/ppermute | solution.py:26
  17.1 1.7 %collective-permute-start.4 = (f32[128,1024]{1,0:T(8,128)S(1)}, f32[128,1024]{1,0:T(8,128)S(1)}, u32[]{:S(2)}, u32[]{:S(2)}) collective-permute-start(f32[128,1024]{1,0:T(8,128)S(1)} %collective-permute-done.2.refs_2_), channel_id=1, source_target_pairs={{0,1},{1,0},{2,3},{3,2},{4,5},{5,4},{6,7},{7,6},{8,9},{9,8},{10,11... | collective-permute-start | bytes 1572872 | tf_op jit(solution)/shard_map/ppermute | solution.py:26
  18.8 0.7 collective-permute-start.17
  19.5 1.6 %broadcast_in_dim.2 = f32[8,64,1024]{2,1,0:T(8,128)} broadcast(f32[64,1024]{1,0:T(8,128)S(1)} %collective-permute-done.17), dimensions={1,2} | broadcast | bytes 2359296 | tf_op jit(solution)/shard_map/broadcast_in_dim | solution.py:203
  21.1 21.5 %all-to-all-start = ((f32[8,64,1024]{2,1,0:T(8,128)}), f32[8,64,1024]{2,1,0:T(8,128)S(1)}, u32[]{:S(2)}, u32[]{:S(2)}) async-start(f32[8,64,1024]{2,1,0:T(8,128)} %broadcast_in_dim.2), calls=%async_computation | async-start | bytes 4194304 | tf_op jit(solution)/shard_map/all_to_all | solution.py:205
  42.7 10.6 %collective-permute-done.7.refs_7_ = f32[128,1024]{1,0:T(8,128)} collective-permute-done((f32[128,1024]{1,0:T(8,128)}, f32[128,1024]{1,0:T(8,128)}, u32[]{:S(2)}, u32[]{:S(2)}) %collective-permute-start.7) | collective-permute-done | bytes 524320 | tf_op jit(solution)/shard_map/ppermute | solution.py:26
  53.4 0.5 collective-permute-start.8
  53.9 5.0 %collective-permute-done.10.refs_10_ = f32[128,1024]{1,0:T(8,128)S(1)} collective-permute-done((f32[128,1024]{1,0:T(8,128)}, f32[128,1024]{1,0:T(8,128)S(1)}, u32[]{:S(2)}, u32[]{:S(2)}) %collective-permute-start.10) | collective-permute-done | bytes 524320 | tf_op jit(solution)/shard_map/ppermute | solution.py:26
  59.2 0.5 copy-done.6
  59.8 0.8 copy-done.7
  60.7 7.1 %collective-permute-done.refs_1_ = f32[64,1024]{1,0:T(8,128)S(1)} collective-permute-done((f32[64,1024]{1,0:T(8,128)S(1)}, f32[64,1024]{1,0:T(8,128)S(1)}, u32[]{:S(2)}, u32[]{:S(2)}) %collective-permute-start) | collective-permute-done | bytes 262176 | tf_op jit(solution)/shard_map/ppermute | solution.py:26
  67.8 0.7 copy-done.8
  68.5 4.0 %collective-permute-done.14.refs_14_ = f32[64,1024]{1,0:T(8,128)} collective-permute-done((f32[64,1024]{1,0:T(8,128)S(1)}, f32[64,1024]{1,0:T(8,128)}, u32[]{:S(2)}, u32[]{:S(2)}) %collective-permute-start.14) | collective-permute-done | bytes 262176 | tf_op jit(solution)/shard_map/ppermute | solution.py:26
  72.6 0.5 collective-permute-start.12
  73.2 0.8 slice.7
  74.1 3.5 %collective-permute-done.12.refs_12_ = f32[128,1024]{1,0:T(8,128)} collective-permute-done((f32[128,1024]{1,0:T(8,128)S(1)}, f32[128,1024]{1,0:T(8,128)}, u32[]{:S(2)}, u32[]{:S(2)}) %collective-permute-start.12) | collective-permute-done | bytes 524320 | tf_op jit(solution)/shard_map/ppermute | solution.py:26
  77.6 4.2 %collective-permute-done.15.refs_15_ = f32[64,1024]{1,0:T(8,128)S(1)} collective-permute-done((f32[64,1024]{1,0:T(8,128)}, f32[64,1024]{1,0:T(8,128)S(1)}, u32[]{:S(2)}, u32[]{:S(2)}) %collective-permute-start.15) | collective-permute-done | bytes 262176 | tf_op jit(solution)/shard_map/ppermute | solution.py:26
  81.9 0.7 copy-done.9
  82.5 12.7 %shard_map.28 = f32[1024,1024]{1,0:T(8,128)} custom-call(s32[4]{0:T(128)S(1)} %pad_add_fusion.where, s32[256,256]{1,0:T(8,128)} %mask_in.1, f32[64,1024]{1,0:T(8,128)} %refs_0_.1, f32[64,1024]{1,0:T(8,128)} %copy-done.8, f32[128,1024]{1,0:T(8,128)} %copy-done.4, f32[128,1024]{1,0:T(8,128)} %collective-permute-done.3.refs_3_, f32[128,1024]{1,0:T(8,128)} %copy-done.5, ...), custom_call_target="tpu_custom_call" | custom-call | tf_op jit(solution)/shard_map/pallas_call | solution.py:241
  (42 shorter events, 0.9 us)
Async XLA Ops:
  0.0 1.7 %collective-permute-start.1 = (f32[64,1024]{1,0:T(8,128)}, f32[64,1024]{1,0:T(8,128)S(1)}, u32[]{:S(2)}, u32[]{:S(2)}) collective-permute-start(f32[64,1024]{1,0:T(8,128)} %refs_0_.1), channel_id=1, source_target_pairs={{0,1},{1,0},{2,3},{3,2},{4,5},{5,4},{6,7},{7,6},{8,9},{9,8},{10,11... | collective-permute-start | bytes 786440 | tf_op jit(solution)/shard_map/ppermute | solution.py:26
  2.7 11.4 %collective-permute-start.2 = (f32[128,1024]{1,0:T(8,128)S(1)}, f32[128,1024]{1,0:T(8,128)S(1)}, u32[]{:S(2)}, u32[]{:S(2)}) collective-permute-start(f32[128,1024]{1,0:T(8,128)S(1)} %pad_maximum_fusion), channel_id=1, source_target_pairs={{0,32},{1,225},{2,34},{3,227},{4,36},{5,229},{6,38},{7,231},{8,40}... | collective-permute-start | bytes 1572872 | tf_op jit(solution)/shard_map/ppermute | solution.py:26
  3.0 15.8 %collective-permute-start.16 = (f32[64,1024]{1,0:T(8,128)}, f32[64,1024]{1,0:T(8,128)S(1)}, u32[]{:S(2)}, u32[]{:S(2)}) collective-permute-start(f32[64,1024]{1,0:T(8,128)} %refs_0_.1), channel_id=1, source_target_pairs={{0,0},{1,16},{2,2},{3,18},{4,4},{5,20},{6,6},{7,22},{8,8},{9,24},{... | collective-permute-start | bytes 786440 | tf_op jit(solution)/shard_map/ppermute | solution.py:26
  14.1 28.4 %collective-permute-start.6 = (f32[128,1024]{1,0:T(8,128)S(1)}, f32[128,1024]{1,0:T(8,128)}, u32[]{:S(2)}, u32[]{:S(2)}) collective-permute-start(f32[128,1024]{1,0:T(8,128)S(1)} %collective-permute-done.2.refs_2_), channel_id=1, source_target_pairs={{0,32},{1,225},{2,34},{3,227},{4,36},{5,229},{6,38},{7,231},{8,40}... | collective-permute-start | bytes 1572872 | tf_op jit(solution)/shard_map/ppermute | solution.py:26
  14.1 28.4 %collective-permute-start.3 = (f32[128,1024]{1,0:T(8,128)S(1)}, f32[128,1024]{1,0:T(8,128)}, u32[]{:S(2)}, u32[]{:S(2)}) collective-permute-start(f32[128,1024]{1,0:T(8,128)S(1)} %collective-permute-done.2.refs_2_), channel_id=1, source_target_pairs={{0,16},{1,17},{2,18},{3,19},{4,20},{5,21},{6,22},{7,23},{8,24},{9,... | collective-permute-start | bytes 1572872 | tf_op jit(solution)/shard_map/ppermute | solution.py:26
  17.1 25.4 %collective-permute-start.4 = (f32[128,1024]{1,0:T(8,128)S(1)}, f32[128,1024]{1,0:T(8,128)S(1)}, u32[]{:S(2)}, u32[]{:S(2)}) collective-permute-start(f32[128,1024]{1,0:T(8,128)S(1)} %collective-permute-done.2.refs_2_), channel_id=1, source_target_pairs={{0,1},{1,0},{2,3},{3,2},{4,5},{5,4},{6,7},{7,6},{8,9},{9,8},{10,11... | collective-permute-start | bytes 1572872 | tf_op jit(solution)/shard_map/ppermute | solution.py:26
  18.8 0.7 collective-permute-start.17
  21.1 37.9 %copy-start.3 = (f32[64,1024]{1,0:T(8,128)S(1)}, f32[64,1024]{1,0:T(8,128)}, u32[]{:S(2)}) copy-start(f32[64,1024]{1,0:T(8,128)} %refs_0_.1) | copy-start | bytes 786436
  21.1 51.4 %all-to-all-start = ((f32[8,64,1024]{2,1,0:T(8,128)}), f32[8,64,1024]{2,1,0:T(8,128)S(1)}, u32[]{:S(2)}, u32[]{:S(2)}) async-start(f32[8,64,1024]{2,1,0:T(8,128)} %broadcast_in_dim.2), calls=%async_computation | async-start | bytes 4194304 | tf_op jit(solution)/shard_map/all_to_all | solution.py:205
  42.6 16.3 %copy-start.5 = (f32[128,1024]{1,0:T(8,128)}, f32[128,1024]{1,0:T(8,128)S(1)}, u32[]{:S(2)}) copy-start(f32[128,1024]{1,0:T(8,128)S(1)} %collective-permute-done.4.refs_4_) | copy-start | bytes 1572868
  42.6 10.8 %collective-permute-start.7 = (f32[128,1024]{1,0:T(8,128)}, f32[128,1024]{1,0:T(8,128)}, u32[]{:S(2)}, u32[]{:S(2)}) collective-permute-start(f32[128,1024]{1,0:T(8,128)} %collective-permute-done.3.refs_3_), channel_id=1, source_target_pairs={{0,32},{1,225},{2,34},{3,227},{4,36},{5,229},{6,38},{7,231},{8,40}... | collective-permute-start | bytes 1572872 | tf_op jit(solution)/shard_map/ppermute | solution.py:26
  42.7 16.2 %collective-permute-start.10 = (f32[128,1024]{1,0:T(8,128)}, f32[128,1024]{1,0:T(8,128)S(1)}, u32[]{:S(2)}, u32[]{:S(2)}) collective-permute-start(f32[128,1024]{1,0:T(8,128)} %collective-permute-done.6.refs_6_), channel_id=1, source_target_pairs={{0,32},{1,225},{2,34},{3,227},{4,36},{5,229},{6,38},{7,231},{8,40}... | collective-permute-start | bytes 1572872 | tf_op jit(solution)/shard_map/ppermute | solution.py:26
  53.3 5.5 %collective-permute-start.9 = (f32[128,1024]{1,0:T(8,128)}, f32[128,1024]{1,0:T(8,128)S(1)}, u32[]{:S(2)}, u32[]{:S(2)}) collective-permute-start(f32[128,1024]{1,0:T(8,128)} %collective-permute-done.7.refs_7_), channel_id=1, source_target_pairs={{0,1},{1,0},{2,3},{3,2},{4,5},{5,4},{6,7},{7,6},{8,9},{9,8},{10,11... | collective-permute-start | bytes 1572872 | tf_op jit(solution)/shard_map/ppermute | solution.py:26
  53.4 6.4 %collective-permute-start.8 = (f32[128,1024]{1,0:T(8,128)}, f32[128,1024]{1,0:T(8,128)S(1)}, u32[]{:S(2)}, u32[]{:S(2)}) collective-permute-start(f32[128,1024]{1,0:T(8,128)} %collective-permute-done.6.refs_6_), channel_id=1, source_target_pairs={{0,1},{1,0},{2,3},{3,2},{4,5},{5,4},{6,7},{7,6},{8,9},{9,8},{10,11... | collective-permute-start | bytes 1572872 | tf_op jit(solution)/shard_map/ppermute | solution.py:26
  53.9 6.7 %collective-permute-start.5 = (f32[128,1024]{1,0:T(8,128)}, f32[128,1024]{1,0:T(8,128)}, u32[]{:S(2)}, u32[]{:S(2)}) collective-permute-start(f32[128,1024]{1,0:T(8,128)} %collective-permute-done.3.refs_3_), channel_id=1, source_target_pairs={{0,1},{1,0},{2,3},{3,2},{4,5},{5,4},{6,7},{7,6},{8,9},{9,8},{10,11... | collective-permute-start | bytes 1572872 | tf_op jit(solution)/shard_map/ppermute | solution.py:26
  58.9 23.0 %copy-start.1 = (f32[128,1024]{1,0:T(8,128)}, f32[128,1024]{1,0:T(8,128)S(1)}, u32[]{:S(2)}) copy-start(f32[128,1024]{1,0:T(8,128)S(1)} %collective-permute-done.10.refs_10_) | copy-start | bytes 1572868
  58.9 13.6 %collective-permute-start.11 = (f32[128,1024]{1,0:T(8,128)}, f32[128,1024]{1,0:T(8,128)S(1)}, u32[]{:S(2)}, u32[]{:S(2)}) collective-permute-start(f32[128,1024]{1,0:T(8,128)} %collective-permute-done.7.refs_7_), channel_id=1, source_target_pairs={{0,32},{1,225},{2,34},{3,227},{4,36},{5,229},{6,38},{7,231},{8,40}... | collective-permute-start | bytes 1572872 | tf_op jit(solution)/shard_map/ppermute | solution.py:26
  59.0 8.8 %collective-permute-start = (f32[64,1024]{1,0:T(8,128)S(1)}, f32[64,1024]{1,0:T(8,128)S(1)}, u32[]{:S(2)}, u32[]{:S(2)}) collective-permute-start(f32[64,1024]{1,0:T(8,128)S(1)} %copy-done.3), channel_id=1, source_target_pairs={{0,16},{1,17},{2,18},{3,19},{4,20},{5,21},{6,22},{7,23},{8,24},{9,... | collective-permute-start | bytes 786440 | tf_op jit(solution)/shard_map/ppermute | solution.py:26
  60.6 11.9 %collective-permute-start.14 = (f32[64,1024]{1,0:T(8,128)S(1)}, f32[64,1024]{1,0:T(8,128)}, u32[]{:S(2)}, u32[]{:S(2)}) collective-permute-start(f32[64,1024]{1,0:T(8,128)S(1)} %slice.6), channel_id=1, source_target_pairs={{0,32},{1,225},{2,34},{3,227},{4,36},{5,229},{6,38},{7,231},{8,40}... | collective-permute-start | bytes 786440 | tf_op jit(solution)/shard_map/ppermute | solution.py:26
  72.5 9.4 %copy-start.2 = (f32[128,1024]{1,0:T(8,128)}, f32[128,1024]{1,0:T(8,128)S(1)}, u32[]{:S(2)}) copy-start(f32[128,1024]{1,0:T(8,128)S(1)} %collective-permute-done.11.refs_11_) | copy-start | bytes 1572868
  72.5 9.3 %collective-permute-start.18 = (f32[512,1024]{1,0:T(8,128)S(1)}, f32[512,1024]{1,0:T(8,128)}, u32[]{:S(2)}, u32[]{:S(2)}) collective-permute-start(f32[512,1024]{1,0:T(8,128)S(1)} %bitcast.5), channel_id=1, source_target_pairs={{0,1},{1,0},{2,3},{3,2},{4,5},{5,4},{6,7},{7,6},{8,9},{9,8},{10,11... | collective-permute-start | bytes 6291464 | tf_op jit(solution)/shard_map/ppermute | solution.py:26
  72.6 5.0 %collective-permute-start.12 = (f32[128,1024]{1,0:T(8,128)S(1)}, f32[128,1024]{1,0:T(8,128)}, u32[]{:S(2)}, u32[]{:S(2)}) collective-permute-start(f32[128,1024]{1,0:T(8,128)S(1)} %collective-permute-done.10.refs_10_), channel_id=1, source_target_pairs={{0,1},{1,0},{2,3},{3,2},{4,5},{5,4},{6,7},{7,6},{8,9},{9,8},{10,11... | collective-permute-start | bytes 1572872 | tf_op jit(solution)/shard_map/ppermute | solution.py:26
  73.1 8.7 %collective-permute-start.13 = (f32[128,1024]{1,0:T(8,128)S(1)}, f32[128,1024]{1,0:T(8,128)}, u32[]{:S(2)}, u32[]{:S(2)}) collective-permute-start(f32[128,1024]{1,0:T(8,128)S(1)} %collective-permute-done.11.refs_11_), channel_id=1, source_target_pairs={{0,1},{1,0},{2,3},{3,2},{4,5},{5,4},{6,7},{7,6},{8,9},{9,8},{10,11... | collective-permute-start | bytes 1572872 | tf_op jit(solution)/shard_map/ppermute | solution.py:26
  74.0 7.8 %collective-permute-start.15 = (f32[64,1024]{1,0:T(8,128)}, f32[64,1024]{1,0:T(8,128)S(1)}, u32[]{:S(2)}, u32[]{:S(2)}) collective-permute-start(f32[64,1024]{1,0:T(8,128)} %slice.7), channel_id=1, source_target_pairs={{0,32},{1,225},{2,34},{3,227},{4,36},{5,229},{6,38},{7,231},{8,40}... | collective-permute-start | bytes 786440 | tf_op jit(solution)/shard_map/ppermute | solution.py:26
  (6 other events, 19.5 us)

commit v3 on v2

--- a/solution.py
+++ b/solution.py
@@ -198,7 +198,7 @@
     a1 = along_z(own_pair)
     partner = other_xh(after(own, own))
     mine = to_rows(spread)
-    a2 = along_z(after(a1, a1))
+    a2 = along_z(after(a1, mine))
     b1 = other_xh(after(a1, a1))
     copies = jnp.broadcast_to(after(mine, mine)[None], (NM, n, cols))
     groups = [[2 * line + k for line in range(NM)] for k in range(2)]

time: 96 us -> 93.7 us (0.976); the launches traced: 95.4 us -> 92 us
  waiting for transfers between devices: 45.6 us -> 41.9 us
    ppermute x19, starting transfers between devices: 8.99 us -> 24.6 us  [permute(): return lax.ppermute(value, AXES, pairs)]
    all_to_all x1, starting transfers between devices: 21.5 us -> 6.7 us  [local(): lax.all_to_all(copies, 'col', split_axis=0, concat_axis=0, tiled=True, ax...]
    ppermute x19, waiting for transfers between devices: 45.6 us -> 41.9 us  [permute(): return lax.ppermute(value, AXES, pairs)]
  transfers between devices with their start and end apart: 20 -> 20, of which waited for: 8 -> 7; matrix products, arithmetic and copies ran while one was open for 3% -> 4% of each run, Pallas kernels for 0% -> 0%
where the time goes in v3:
time: 93.7 us; the launch traced here: 92 us
  waiting for transfers between devices  41.9 us (45%)
  starting transfers between devices  31.3 us (33%)
  Pallas kernels  12.7 us (14%)
  local copies, waits for them, and re-layouts  4.65 us (5%)
  other arithmetic  1.07 us (1%)
    ppermute x19, waiting for transfers between devices, permute(): return lax.ppermute(value, AXES, pairs)  41.9 us
    ppermute x19, starting transfers between devices, permute(): return lax.ppermute(value, AXES, pairs)  24.6 us
    pallas_call x1, Pallas kernels, local(): pl.pallas_call(functools.partial(kernel, moves, len(arrays)), out_shape=j...  12.7 us
    all_to_all x1, starting transfers between devices, local(): lax.all_to_all(copies, 'col', split_axis=0, concat_axis=0, tiled=True, ax...  6.7 us
    unnamed x20, local copies, waits for them, and re-layouts  2.21 us
  transfers between devices with their start and end apart: 20, of which 7 were waited for; matrix products, arithmetic and copies ran while one was open for 4% of the time, Pallas kernels for 0%

profile of v3, /device:TPU:0, one launch (start us, length us, event | category | flops | bytes accessed | tf_op | source)
XLA Modules:
  0.0 92.0 jit_solution(1666090032762651154)
XLA Ops:
  0.0 1.6 %collective-permute-start.6 = (f32[64,1024]{1,0:T(8,128)}, f32[64,1024]{1,0:T(8,128)S(1)}, u32[]{:S(2)}, u32[]{:S(2)}) collective-permute-start(f32[64,1024]{1,0:T(8,128)} %refs_0_.1), channel_id=1, source_target_pairs={{0,0},{1,16},{2,2},{3,18},{4,4},{5,20},{6,6},{7,22},{8,8},{9,24},{... | collective-permute-start | bytes 786440 | tf_op jit(solution)/shard_map/ppermute | solution.py:26
  1.7 1.0 %pad_maximum_fusion = f32[128,1024]{1,0:T(8,128)S(1)} fusion(f32[64,1024]{1,0:T(8,128)S(1)} %collective-permute-done.1, f32[64,1024]{1,0:T(8,128)} %refs_0_.1), kind=kLoop, calls=%fused_computation | loop fusion | flops 131072 | bytes 1048576 | tf_op jit(solution)/shard_map/concatenate | solution.py:193
  2.7 2.0 %collective-permute-start.2 = (f32[128,1024]{1,0:T(8,128)S(1)}, f32[128,1024]{1,0:T(8,128)S(1)}, u32[]{:S(2)}, u32[]{:S(2)}) collective-permute-start(f32[128,1024]{1,0:T(8,128)S(1)} %pad_maximum_fusion), channel_id=1, source_target_pairs={{0,32},{1,225},{2,34},{3,227},{4,36},{5,229},{6,38},{7,231},{8,40}... | collective-permute-start | bytes 1572872 | tf_op jit(solution)/shard_map/ppermute | solution.py:26
  4.7 0.7 collective-permute-start.7
  5.4 12.9 %collective-permute-done.2.refs_2_ = f32[128,1024]{1,0:T(8,128)S(1)} collective-permute-done((f32[128,1024]{1,0:T(8,128)S(1)}, f32[128,1024]{1,0:T(8,128)S(1)}, u32[]{:S(2)}, u32[]{:S(2)}) %collective-permute-start.2) | collective-permute-done | bytes 524320 | tf_op jit(solution)/shard_map/ppermute | solution.py:26
  18.3 0.7 collective-permute-start.3
  19.0 8.1 %collective-permute-start.8 = (f32[128,1024]{1,0:T(8,128)S(1)}, f32[128,1024]{1,0:T(8,128)}, u32[]{:S(2)}, u32[]{:S(2)}) collective-permute-start(f32[128,1024]{1,0:T(8,128)S(1)} %collective-permute-done.2.refs_2_), channel_id=1, source_target_pairs={{0,32},{1,225},{2,34},{3,227},{4,36},{5,229},{6,38},{7,231},{8,40}... | collective-permute-start | bytes 1572872 | tf_op jit(solution)/shard_map/ppermute | solution.py:26
  27.1 2.4 %collective-permute-start.4 = (f32[128,1024]{1,0:T(8,128)S(1)}, f32[128,1024]{1,0:T(8,128)S(1)}, u32[]{:S(2)}, u32[]{:S(2)}) collective-permute-start(f32[128,1024]{1,0:T(8,128)S(1)} %collective-permute-done.2.refs_2_), channel_id=1, source_target_pairs={{0,1},{1,0},{2,3},{3,2},{4,5},{5,4},{6,7},{7,6},{8,9},{9,8},{10,11... | collective-permute-start | bytes 1572872 | tf_op jit(solution)/shard_map/ppermute | solution.py:26
  29.4 1.6 %broadcast_in_dim.2 = f32[8,64,1024]{2,1,0:T(8,128)} broadcast(f32[64,1024]{1,0:T(8,128)S(1)} %collective-permute-done.7), dimensions={1,2} | broadcast | bytes 2359296 | tf_op jit(solution)/shard_map/broadcast_in_dim | solution.py:203
  31.0 6.7 %all-to-all-start = ((f32[8,64,1024]{2,1,0:T(8,128)}), f32[8,64,1024]{2,1,0:T(8,128)S(1)}, u32[]{:S(2)}, u32[]{:S(2)}) async-start(f32[8,64,1024]{2,1,0:T(8,128)} %broadcast_in_dim.2), calls=%async_computation | async-start | bytes 4194304 | tf_op jit(solution)/shard_map/all_to_all | solution.py:205
  37.8 1.1 %collective-permute-start.9 = (f32[128,1024]{1,0:T(8,128)}, f32[128,1024]{1,0:T(8,128)}, u32[]{:S(2)}, u32[]{:S(2)}) collective-permute-start(f32[128,1024]{1,0:T(8,128)} %collective-permute-done.3.refs_3_), channel_id=1, source_target_pairs={{0,32},{1,225},{2,34},{3,227},{4,36},{5,229},{6,38},{7,231},{8,40}... | collective-permute-start | bytes 1572872 | tf_op jit(solution)/shard_map/ppermute | solution.py:26
  38.9 2.6 %collective-permute-start.12 = (f32[128,1024]{1,0:T(8,128)}, f32[128,1024]{1,0:T(8,128)S(1)}, u32[]{:S(2)}, u32[]{:S(2)}) collective-permute-start(f32[128,1024]{1,0:T(8,128)} %collective-permute-done.8.refs_6_), channel_id=1, source_target_pairs={{0,32},{1,225},{2,34},{3,227},{4,36},{5,229},{6,38},{7,231},{8,40}... | collective-permute-start | bytes 1572872 | tf_op jit(solution)/shard_map/ppermute | solution.py:26
  41.5 7.1 %collective-permute-done.9.refs_7_ = f32[128,1024]{1,0:T(8,128)} collective-permute-done((f32[128,1024]{1,0:T(8,128)}, f32[128,1024]{1,0:T(8,128)}, u32[]{:S(2)}, u32[]{:S(2)}) %collective-permute-start.9) | collective-permute-done | bytes 524320 | tf_op jit(solution)/shard_map/ppermute | solution.py:26
  49.1 5.0 %collective-permute-done.12.refs_10_ = f32[128,1024]{1,0:T(8,128)S(1)} collective-permute-done((f32[128,1024]{1,0:T(8,128)}, f32[128,1024]{1,0:T(8,128)S(1)}, u32[]{:S(2)}, u32[]{:S(2)}) %collective-permute-start.12) | collective-permute-done | bytes 524320 | tf_op jit(solution)/shard_map/ppermute | solution.py:26
  54.2 1.6 %collective-permute-start = (f32[64,1024]{1,0:T(8,128)S(1)}, f32[64,1024]{1,0:T(8,128)S(1)}, u32[]{:S(2)}, u32[]{:S(2)}) collective-permute-start(f32[64,1024]{1,0:T(8,128)S(1)} %copy-done.3), channel_id=1, source_target_pairs={{0,16},{1,17},{2,18},{3,19},{4,20},{5,21},{6,22},{7,23},{8,24},{9,... | collective-permute-start | bytes 786440 | tf_op jit(solution)/shard_map/ppermute | solution.py:26
  55.8 0.8 copy-done.7
  56.6 2.5 %collective-permute-start.16 = (f32[64,1024]{1,0:T(8,128)S(1)}, f32[64,1024]{1,0:T(8,128)}, u32[]{:S(2)}, u32[]{:S(2)}) collective-permute-start(f32[64,1024]{1,0:T(8,128)S(1)} %slice.6), channel_id=1, source_target_pairs={{0,32},{1,225},{2,34},{3,227},{4,36},{5,229},{6,38},{7,231},{8,40}... | collective-permute-start | bytes 786440 | tf_op jit(solution)/shard_map/ppermute | solution.py:26
  59.1 9.2 %collective-permute-done.refs_1_ = f32[64,1024]{1,0:T(8,128)S(1)} collective-permute-done((f32[64,1024]{1,0:T(8,128)S(1)}, f32[64,1024]{1,0:T(8,128)S(1)}, u32[]{:S(2)}, u32[]{:S(2)}) %collective-permute-start) | collective-permute-done | bytes 262176 | tf_op jit(solution)/shard_map/ppermute | solution.py:26
  68.3 0.7 copy-done.8
  69.7 0.8 slice.7
  70.8 3.4 %collective-permute-done.14.refs_12_ = f32[128,1024]{1,0:T(8,128)} collective-permute-done((f32[128,1024]{1,0:T(8,128)S(1)}, f32[128,1024]{1,0:T(8,128)}, u32[]{:S(2)}, u32[]{:S(2)}) %collective-permute-start.14) | collective-permute-done | bytes 524320 | tf_op jit(solution)/shard_map/ppermute | solution.py:26
  74.2 4.2 %collective-permute-done.17.refs_15_ = f32[64,1024]{1,0:T(8,128)S(1)} collective-permute-done((f32[64,1024]{1,0:T(8,128)}, f32[64,1024]{1,0:T(8,128)S(1)}, u32[]{:S(2)}, u32[]{:S(2)}) %collective-permute-start.17) | collective-permute-done | bytes 262176 | tf_op jit(solution)/shard_map/ppermute | solution.py:26
  78.4 0.7 copy-done.9
  79.1 12.7 %shard_map.28 = f32[1024,1024]{1,0:T(8,128)} custom-call(s32[4]{0:T(128)S(1)} %pad_add_fusion.where, s32[256,256]{1,0:T(8,128)} %mask_in.1, f32[64,1024]{1,0:T(8,128)} %refs_0_.1, f32[64,1024]{1,0:T(8,128)} %copy-done.8, f32[128,1024]{1,0:T(8,128)} %copy-done.4, f32[128,1024]{1,0:T(8,128)} %collective-permute-done.3.refs_3_, f32[128,1024]{1,0:T(8,128)} %copy-done.5, ...), custom_call_target="tpu_custom_call" | custom-call | tf_op jit(solution)/shard_map/pallas_call | solution.py:241
  (42 shorter events, 1.7 us)
Async XLA Ops:
  0.0 1.7 %collective-permute-start.1 = (f32[64,1024]{1,0:T(8,128)}, f32[64,1024]{1,0:T(8,128)S(1)}, u32[]{:S(2)}, u32[]{:S(2)}) collective-permute-start(f32[64,1024]{1,0:T(8,128)} %refs_0_.1), channel_id=1, source_target_pairs={{0,1},{1,0},{2,3},{3,2},{4,5},{5,4},{6,7},{7,6},{8,9},{9,8},{10,11... | collective-permute-start | bytes 786440 | tf_op jit(solution)/shard_map/ppermute | solution.py:26
  0.0 4.7 %collective-permute-start.6 = (f32[64,1024]{1,0:T(8,128)}, f32[64,1024]{1,0:T(8,128)S(1)}, u32[]{:S(2)}, u32[]{:S(2)}) collective-permute-start(f32[64,1024]{1,0:T(8,128)} %refs_0_.1), channel_id=1, source_target_pairs={{0,0},{1,16},{2,2},{3,18},{4,4},{5,20},{6,6},{7,22},{8,8},{9,24},{... | collective-permute-start | bytes 786440 | tf_op jit(solution)/shard_map/ppermute | solution.py:26
  2.7 15.5 %collective-permute-start.2 = (f32[128,1024]{1,0:T(8,128)S(1)}, f32[128,1024]{1,0:T(8,128)S(1)}, u32[]{:S(2)}, u32[]{:S(2)}) collective-permute-start(f32[128,1024]{1,0:T(8,128)S(1)} %pad_maximum_fusion), channel_id=1, source_target_pairs={{0,32},{1,225},{2,34},{3,227},{4,36},{5,229},{6,38},{7,231},{8,40}... | collective-permute-start | bytes 1572872 | tf_op jit(solution)/shard_map/ppermute | solution.py:26
  4.7 0.7 collective-permute-start.7
  18.3 12.8 %copy-start.4 = (f32[128,1024]{1,0:T(8,128)}, f32[128,1024]{1,0:T(8,128)S(1)}, u32[]{:S(2)}) copy-start(f32[128,1024]{1,0:T(8,128)S(1)} %collective-permute-done.2.refs_2_) | copy-start | bytes 1572868
  18.3 19.5 %collective-permute-start.3 = (f32[128,1024]{1,0:T(8,128)S(1)}, f32[128,1024]{1,0:T(8,128)}, u32[]{:S(2)}, u32[]{:S(2)}) collective-permute-start(f32[128,1024]{1,0:T(8,128)S(1)} %collective-permute-done.2.refs_2_), channel_id=1, source_target_pairs={{0,16},{1,17},{2,18},{3,19},{4,20},{5,21},{6,22},{7,23},{8,24},{9,... | collective-permute-start | bytes 1572872 | tf_op jit(solution)/shard_map/ppermute | solution.py:26
  19.0 18.7 %collective-permute-start.8 = (f32[128,1024]{1,0:T(8,128)S(1)}, f32[128,1024]{1,0:T(8,128)}, u32[]{:S(2)}, u32[]{:S(2)}) collective-permute-start(f32[128,1024]{1,0:T(8,128)S(1)} %collective-permute-done.2.refs_2_), channel_id=1, source_target_pairs={{0,32},{1,225},{2,34},{3,227},{4,36},{5,229},{6,38},{7,231},{8,40}... | collective-permute-start | bytes 1572872 | tf_op jit(solution)/shard_map/ppermute | solution.py:26
  27.1 10.7 %collective-permute-start.4 = (f32[128,1024]{1,0:T(8,128)S(1)}, f32[128,1024]{1,0:T(8,128)S(1)}, u32[]{:S(2)}, u32[]{:S(2)}) collective-permute-start(f32[128,1024]{1,0:T(8,128)S(1)} %collective-permute-done.2.refs_2_), channel_id=1, source_target_pairs={{0,1},{1,0},{2,3},{3,2},{4,5},{5,4},{6,7},{7,6},{8,9},{9,8},{10,11... | collective-permute-start | bytes 1572872 | tf_op jit(solution)/shard_map/ppermute | solution.py:26
  31.0 23.2 %copy-start.3 = (f32[64,1024]{1,0:T(8,128)S(1)}, f32[64,1024]{1,0:T(8,128)}, u32[]{:S(2)}) copy-start(f32[64,1024]{1,0:T(8,128)} %refs_0_.1) | copy-start | bytes 786436
  31.0 38.0 %all-to-all-start = ((f32[8,64,1024]{2,1,0:T(8,128)}), f32[8,64,1024]{2,1,0:T(8,128)S(1)}, u32[]{:S(2)}, u32[]{:S(2)}) async-start(f32[8,64,1024]{2,1,0:T(8,128)} %broadcast_in_dim.2), calls=%async_computation | async-start | bytes 4194304 | tf_op jit(solution)/shard_map/all_to_all | solution.py:205
  37.8 16.3 %copy-start.5 = (f32[128,1024]{1,0:T(8,128)}, f32[128,1024]{1,0:T(8,128)S(1)}, u32[]{:S(2)}) copy-start(f32[128,1024]{1,0:T(8,128)S(1)} %collective-permute-done.4.refs_4_) | copy-start | bytes 1572868
  37.8 10.8 %collective-permute-start.9 = (f32[128,1024]{1,0:T(8,128)}, f32[128,1024]{1,0:T(8,128)}, u32[]{:S(2)}, u32[]{:S(2)}) collective-permute-start(f32[128,1024]{1,0:T(8,128)} %collective-permute-done.3.refs_3_), channel_id=1, source_target_pairs={{0,32},{1,225},{2,34},{3,227},{4,36},{5,229},{6,38},{7,231},{8,40}... | collective-permute-start | bytes 1572872 | tf_op jit(solution)/shard_map/ppermute | solution.py:26
  38.9 15.2 %collective-permute-start.12 = (f32[128,1024]{1,0:T(8,128)}, f32[128,1024]{1,0:T(8,128)S(1)}, u32[]{:S(2)}, u32[]{:S(2)}) collective-permute-start(f32[128,1024]{1,0:T(8,128)} %collective-permute-done.8.refs_6_), channel_id=1, source_target_pairs={{0,32},{1,225},{2,34},{3,227},{4,36},{5,229},{6,38},{7,231},{8,40}... | collective-permute-start | bytes 1572872 | tf_op jit(solution)/shard_map/ppermute | solution.py:26
  48.5 5.5 %collective-permute-start.11 = (f32[128,1024]{1,0:T(8,128)}, f32[128,1024]{1,0:T(8,128)S(1)}, u32[]{:S(2)}, u32[]{:S(2)}) collective-permute-start(f32[128,1024]{1,0:T(8,128)} %collective-permute-done.9.refs_7_), channel_id=1, source_target_pairs={{0,1},{1,0},{2,3},{3,2},{4,5},{5,4},{6,7},{7,6},{8,9},{9,8},{10,11... | collective-permute-start | bytes 1572872 | tf_op jit(solution)/shard_map/ppermute | solution.py:26
  48.6 7.2 %collective-permute-start.5 = (f32[128,1024]{1,0:T(8,128)}, f32[128,1024]{1,0:T(8,128)S(1)}, u32[]{:S(2)}, u32[]{:S(2)}) collective-permute-start(f32[128,1024]{1,0:T(8,128)} %collective-permute-done.3.refs_3_), channel_id=1, source_target_pairs={{0,1},{1,0},{2,3},{3,2},{4,5},{5,4},{6,7},{7,6},{8,9},{9,8},{10,11... | collective-permute-start | bytes 1572872 | tf_op jit(solution)/shard_map/ppermute | solution.py:26
  49.1 7.5 %collective-permute-start.10 = (f32[128,1024]{1,0:T(8,128)}, f32[128,1024]{1,0:T(8,128)}, u32[]{:S(2)}, u32[]{:S(2)}) collective-permute-start(f32[128,1024]{1,0:T(8,128)} %collective-permute-done.8.refs_6_), channel_id=1, source_target_pairs={{0,1},{1,0},{2,3},{3,2},{4,5},{5,4},{6,7},{7,6},{8,9},{9,8},{10,11... | collective-permute-start | bytes 1572872 | tf_op jit(solution)/shard_map/ppermute | solution.py:26
  54.1 24.3 %copy-start.1 = (f32[128,1024]{1,0:T(8,128)}, f32[128,1024]{1,0:T(8,128)S(1)}, u32[]{:S(2)}) copy-start(f32[128,1024]{1,0:T(8,128)S(1)} %collective-permute-done.12.refs_10_) | copy-start | bytes 1572868
  54.1 14.9 %collective-permute-start.13 = (f32[128,1024]{1,0:T(8,128)}, f32[128,1024]{1,0:T(8,128)S(1)}, u32[]{:S(2)}, u32[]{:S(2)}) collective-permute-start(f32[128,1024]{1,0:T(8,128)} %collective-permute-done.9.refs_7_), channel_id=1, source_target_pairs={{0,32},{1,225},{2,34},{3,227},{4,36},{5,229},{6,38},{7,231},{8,40}... | collective-permute-start | bytes 1572872 | tf_op jit(solution)/shard_map/ppermute | solution.py:26
  54.2 14.1 %collective-permute-start = (f32[64,1024]{1,0:T(8,128)S(1)}, f32[64,1024]{1,0:T(8,128)S(1)}, u32[]{:S(2)}, u32[]{:S(2)}) collective-permute-start(f32[64,1024]{1,0:T(8,128)S(1)} %copy-done.3), channel_id=1, source_target_pairs={{0,16},{1,17},{2,18},{3,19},{4,20},{5,21},{6,22},{7,23},{8,24},{9,... | collective-permute-start | bytes 786440 | tf_op jit(solution)/shard_map/ppermute | solution.py:26
  56.6 12.4 %collective-permute-start.16 = (f32[64,1024]{1,0:T(8,128)S(1)}, f32[64,1024]{1,0:T(8,128)}, u32[]{:S(2)}, u32[]{:S(2)}) collective-permute-start(f32[64,1024]{1,0:T(8,128)S(1)} %slice.6), channel_id=1, source_target_pairs={{0,32},{1,225},{2,34},{3,227},{4,36},{5,229},{6,38},{7,231},{8,40}... | collective-permute-start | bytes 786440 | tf_op jit(solution)/shard_map/ppermute | solution.py:26
  69.0 9.3 %collective-permute-start.18 = (f32[512,1024]{1,0:T(8,128)S(1)}, f32[512,1024]{1,0:T(8,128)}, u32[]{:S(2)}, u32[]{:S(2)}) collective-permute-start(f32[512,1024]{1,0:T(8,128)S(1)} %bitcast.5), channel_id=1, source_target_pairs={{0,1},{1,0},{2,3},{3,2},{4,5},{5,4},{6,7},{7,6},{8,9},{9,8},{10,11... | collective-permute-start | bytes 6291464 | tf_op jit(solution)/shard_map/ppermute | solution.py:26
  69.1 5.0 %collective-permute-start.14 = (f32[128,1024]{1,0:T(8,128)S(1)}, f32[128,1024]{1,0:T(8,128)}, u32[]{:S(2)}, u32[]{:S(2)}) collective-permute-start(f32[128,1024]{1,0:T(8,128)S(1)} %collective-permute-done.12.refs_10_), channel_id=1, source_target_pairs={{0,1},{1,0},{2,3},{3,2},{4,5},{5,4},{6,7},{7,6},{8,9},{9,8},{10,11... | collective-permute-start | bytes 1572872 | tf_op jit(solution)/shard_map/ppermute | solution.py:26
  69.6 8.7 %collective-permute-start.15 = (f32[128,1024]{1,0:T(8,128)S(1)}, f32[128,1024]{1,0:T(8,128)}, u32[]{:S(2)}, u32[]{:S(2)}) collective-permute-start(f32[128,1024]{1,0:T(8,128)S(1)} %collective-permute-done.13.refs_11_), channel_id=1, source_target_pairs={{0,1},{1,0},{2,3},{3,2},{4,5},{5,4},{6,7},{7,6},{8,9},{9,8},{10,11... | collective-permute-start | bytes 1572872 | tf_op jit(solution)/shard_map/ppermute | solution.py:26
  70.6 7.8 %collective-permute-start.17 = (f32[64,1024]{1,0:T(8,128)}, f32[64,1024]{1,0:T(8,128)S(1)}, u32[]{:S(2)}, u32[]{:S(2)}) collective-permute-start(f32[64,1024]{1,0:T(8,128)} %slice.7), channel_id=1, source_target_pairs={{0,32},{1,225},{2,34},{3,227},{4,36},{5,229},{6,38},{7,231},{8,40}... | collective-permute-start | bytes 786440 | tf_op jit(solution)/shard_map/ppermute | solution.py:26
  (6 other events, 22.7 us)

commit v4 on v3

--- a/solution.py
+++ b/solution.py
@@ -261,7 +261,7 @@
             pltpu.SemaphoreType.DMA,
             pltpu.SemaphoreType.DMA((cols // STRIPE,)),
         ],
-        compiler_params=pltpu.CompilerParams(vmem_limit_bytes=32 * 1024 * 1024),
+        compiler_params=pltpu.CompilerParams(vmem_limit_bytes=26 * 1024 * 1024),
     )(where, pltpu.with_memory_space_constraint(tile_mask, pltpu.HBM), *arrays)
 
 

time: 93.7 us -> 93.7 us (level)
  no operation moved by 1% of the time
where the time goes in v4:
time: 93.7 us; the launch traced here: 92 us
  waiting for transfers between devices  41.9 us (45%)
  starting transfers between devices  31.3 us (33%)
  Pallas kernels  12.7 us (14%)
  local copies, waits for them, and re-layouts  4.65 us (5%)
  other arithmetic  1.07 us (1%)
    ppermute x19, waiting for transfers between devices, permute(): return lax.ppermute(value, AXES, pairs)  41.9 us
    ppermute x19, starting transfers between devices, permute(): return lax.ppermute(value, AXES, pairs)  24.6 us
    pallas_call x1, Pallas kernels, local(): pl.pallas_call(functools.partial(kernel, moves, len(arrays)), out_shape=j...  12.7 us
    all_to_all x1, starting transfers between devices, local(): lax.all_to_all(copies, 'col', split_axis=0, concat_axis=0, tiled=True, ax...  6.7 us
    unnamed x20, local copies, waits for them, and re-layouts  2.21 us
  transfers between devices with their start and end apart: 20, of which 7 were waited for; matrix products, arithmetic and copies ran while one was open for 4% of the time, Pallas kernels for 0%

profile of v4, /device:TPU:0, one launch (start us, length us, event | category | flops | bytes accessed | tf_op | source)
XLA Modules:
  0.0 92.0 jit_solution(13342408865528516630)
XLA Ops:
  0.0 1.6 %collective-permute-start.6 = (f32[64,1024]{1,0:T(8,128)}, f32[64,1024]{1,0:T(8,128)S(1)}, u32[]{:S(2)}, u32[]{:S(2)}) collective-permute-start(f32[64,1024]{1,0:T(8,128)} %refs_0_.1), channel_id=1, source_target_pairs={{0,0},{1,16},{2,2},{3,18},{4,4},{5,20},{6,6},{7,22},{8,8},{9,24},{... | collective-permute-start | bytes 786440 | tf_op jit(solution)/shard_map/ppermute | solution.py:26
  1.7 1.0 %pad_maximum_fusion = f32[128,1024]{1,0:T(8,128)S(1)} fusion(f32[64,1024]{1,0:T(8,128)S(1)} %collective-permute-done.1, f32[64,1024]{1,0:T(8,128)} %refs_0_.1), kind=kLoop, calls=%fused_computation | loop fusion | flops 131072 | bytes 1048576 | tf_op jit(solution)/shard_map/concatenate | solution.py:193
  2.7 2.0 %collective-permute-start.2 = (f32[128,1024]{1,0:T(8,128)S(1)}, f32[128,1024]{1,0:T(8,128)S(1)}, u32[]{:S(2)}, u32[]{:S(2)}) collective-permute-start(f32[128,1024]{1,0:T(8,128)S(1)} %pad_maximum_fusion), channel_id=1, source_target_pairs={{0,32},{1,225},{2,34},{3,227},{4,36},{5,229},{6,38},{7,231},{8,40}... | collective-permute-start | bytes 1572872 | tf_op jit(solution)/shard_map/ppermute | solution.py:26
  4.7 0.7 collective-permute-start.7
  5.4 12.9 %collective-permute-done.2.refs_2_ = f32[128,1024]{1,0:T(8,128)S(1)} collective-permute-done((f32[128,1024]{1,0:T(8,128)S(1)}, f32[128,1024]{1,0:T(8,128)S(1)}, u32[]{:S(2)}, u32[]{:S(2)}) %collective-permute-start.2) | collective-permute-done | bytes 524320 | tf_op jit(solution)/shard_map/ppermute | solution.py:26
  18.3 0.7 collective-permute-start.3
  19.0 8.1 %collective-permute-start.8 = (f32[128,1024]{1,0:T(8,128)S(1)}, f32[128,1024]{1,0:T(8,128)}, u32[]{:S(2)}, u32[]{:S(2)}) collective-permute-start(f32[128,1024]{1,0:T(8,128)S(1)} %collective-permute-done.2.refs_2_), channel_id=1, source_target_pairs={{0,32},{1,225},{2,34},{3,227},{4,36},{5,229},{6,38},{7,231},{8,40}... | collective-permute-start | bytes 1572872 | tf_op jit(solution)/shard_map/ppermute | solution.py:26
  27.1 2.4 %collective-permute-start.4 = (f32[128,1024]{1,0:T(8,128)S(1)}, f32[128,1024]{1,0:T(8,128)S(1)}, u32[]{:S(2)}, u32[]{:S(2)}) collective-permute-start(f32[128,1024]{1,0:T(8,128)S(1)} %collective-permute-done.2.refs_2_), channel_id=1, source_target_pairs={{0,1},{1,0},{2,3},{3,2},{4,5},{5,4},{6,7},{7,6},{8,9},{9,8},{10,11... | collective-permute-start | bytes 1572872 | tf_op jit(solution)/shard_map/ppermute | solution.py:26
  29.4 1.6 %broadcast_in_dim.2 = f32[8,64,1024]{2,1,0:T(8,128)} broadcast(f32[64,1024]{1,0:T(8,128)S(1)} %collective-permute-done.7), dimensions={1,2} | broadcast | bytes 2359296 | tf_op jit(solution)/shard_map/broadcast_in_dim | solution.py:203
  31.0 6.7 %all-to-all-start = ((f32[8,64,1024]{2,1,0:T(8,128)}), f32[8,64,1024]{2,1,0:T(8,128)S(1)}, u32[]{:S(2)}, u32[]{:S(2)}) async-start(f32[8,64,1024]{2,1,0:T(8,128)} %broadcast_in_dim.2), calls=%async_computation | async-start | bytes 4194304 | tf_op jit(solution)/shard_map/all_to_all | solution.py:205
  37.8 1.1 %collective-permute-start.9 = (f32[128,1024]{1,0:T(8,128)}, f32[128,1024]{1,0:T(8,128)}, u32[]{:S(2)}, u32[]{:S(2)}) collective-permute-start(f32[128,1024]{1,0:T(8,128)} %collective-permute-done.3.refs_3_), channel_id=1, source_target_pairs={{0,32},{1,225},{2,34},{3,227},{4,36},{5,229},{6,38},{7,231},{8,40}... | collective-permute-start | bytes 1572872 | tf_op jit(solution)/shard_map/ppermute | solution.py:26
  38.9 2.6 %collective-permute-start.12 = (f32[128,1024]{1,0:T(8,128)}, f32[128,1024]{1,0:T(8,128)S(1)}, u32[]{:S(2)}, u32[]{:S(2)}) collective-permute-start(f32[128,1024]{1,0:T(8,128)} %collective-permute-done.8.refs_6_), channel_id=1, source_target_pairs={{0,32},{1,225},{2,34},{3,227},{4,36},{5,229},{6,38},{7,231},{8,40}... | collective-permute-start | bytes 1572872 | tf_op jit(solution)/shard_map/ppermute | solution.py:26
  41.5 7.1 %collective-permute-done.9.refs_7_ = f32[128,1024]{1,0:T(8,128)} collective-permute-done((f32[128,1024]{1,0:T(8,128)}, f32[128,1024]{1,0:T(8,128)}, u32[]{:S(2)}, u32[]{:S(2)}) %collective-permute-start.9) | collective-permute-done | bytes 524320 | tf_op jit(solution)/shard_map/ppermute | solution.py:26
  49.1 5.0 %collective-permute-done.12.refs_10_ = f32[128,1024]{1,0:T(8,128)S(1)} collective-permute-done((f32[128,1024]{1,0:T(8,128)}, f32[128,1024]{1,0:T(8,128)S(1)}, u32[]{:S(2)}, u32[]{:S(2)}) %collective-permute-start.12) | collective-permute-done | bytes 524320 | tf_op jit(solution)/shard_map/ppermute | solution.py:26
  54.2 1.6 %collective-permute-start = (f32[64,1024]{1,0:T(8,128)S(1)}, f32[64,1024]{1,0:T(8,128)S(1)}, u32[]{:S(2)}, u32[]{:S(2)}) collective-permute-start(f32[64,1024]{1,0:T(8,128)S(1)} %copy-done.3), channel_id=1, source_target_pairs={{0,16},{1,17},{2,18},{3,19},{4,20},{5,21},{6,22},{7,23},{8,24},{9,... | collective-permute-start | bytes 786440 | tf_op jit(solution)/shard_map/ppermute | solution.py:26
  55.8 0.8 copy-done.7
  56.6 2.5 %collective-permute-start.16 = (f32[64,1024]{1,0:T(8,128)S(1)}, f32[64,1024]{1,0:T(8,128)}, u32[]{:S(2)}, u32[]{:S(2)}) collective-permute-start(f32[64,1024]{1,0:T(8,128)S(1)} %slice.6), channel_id=1, source_target_pairs={{0,32},{1,225},{2,34},{3,227},{4,36},{5,229},{6,38},{7,231},{8,40}... | collective-permute-start | bytes 786440 | tf_op jit(solution)/shard_map/ppermute | solution.py:26
  59.1 9.2 %collective-permute-done.refs_1_ = f32[64,1024]{1,0:T(8,128)S(1)} collective-permute-done((f32[64,1024]{1,0:T(8,128)S(1)}, f32[64,1024]{1,0:T(8,128)S(1)}, u32[]{:S(2)}, u32[]{:S(2)}) %collective-permute-start) | collective-permute-done | bytes 262176 | tf_op jit(solution)/shard_map/ppermute | solution.py:26
  68.3 0.7 copy-done.8
  69.7 0.8 slice.7
  70.8 3.4 %collective-permute-done.14.refs_12_ = f32[128,1024]{1,0:T(8,128)} collective-permute-done((f32[128,1024]{1,0:T(8,128)S(1)}, f32[128,1024]{1,0:T(8,128)}, u32[]{:S(2)}, u32[]{:S(2)}) %collective-permute-start.14) | collective-permute-done | bytes 524320 | tf_op jit(solution)/shard_map/ppermute | solution.py:26
  74.2 4.2 %collective-permute-done.17.refs_15_ = f32[64,1024]{1,0:T(8,128)S(1)} collective-permute-done((f32[64,1024]{1,0:T(8,128)}, f32[64,1024]{1,0:T(8,128)S(1)}, u32[]{:S(2)}, u32[]{:S(2)}) %collective-permute-start.17) | collective-permute-done | bytes 262176 | tf_op jit(solution)/shard_map/ppermute | solution.py:26
  78.4 0.7 copy-done.9
  79.1 12.7 %shard_map.28 = f32[1024,1024]{1,0:T(8,128)} custom-call(s32[4]{0:T(128)S(1)} %pad_add_fusion.where, s32[256,256]{1,0:T(8,128)} %mask_in.1, f32[64,1024]{1,0:T(8,128)} %refs_0_.1, f32[64,1024]{1,0:T(8,128)} %copy-done.8, f32[128,1024]{1,0:T(8,128)} %copy-done.4, f32[128,1024]{1,0:T(8,128)} %collective-permute-done.3.refs_3_, f32[128,1024]{1,0:T(8,128)} %copy-done.5, ...), custom_call_target="tpu_custom_call" | custom-call | tf_op jit(solution)/shard_map/pallas_call | solution.py:241
  (42 shorter events, 1.7 us)
Async XLA Ops:
  0.0 1.7 %collective-permute-start.1 = (f32[64,1024]{1,0:T(8,128)}, f32[64,1024]{1,0:T(8,128)S(1)}, u32[]{:S(2)}, u32[]{:S(2)}) collective-permute-start(f32[64,1024]{1,0:T(8,128)} %refs_0_.1), channel_id=1, source_target_pairs={{0,1},{1,0},{2,3},{3,2},{4,5},{5,4},{6,7},{7,6},{8,9},{9,8},{10,11... | collective-permute-start | bytes 786440 | tf_op jit(solution)/shard_map/ppermute | solution.py:26
  0.0 4.7 %collective-permute-start.6 = (f32[64,1024]{1,0:T(8,128)}, f32[64,1024]{1,0:T(8,128)S(1)}, u32[]{:S(2)}, u32[]{:S(2)}) collective-permute-start(f32[64,1024]{1,0:T(8,128)} %refs_0_.1), channel_id=1, source_target_pairs={{0,0},{1,16},{2,2},{3,18},{4,4},{5,20},{6,6},{7,22},{8,8},{9,24},{... | collective-permute-start | bytes 786440 | tf_op jit(solution)/shard_map/ppermute | solution.py:26
  2.7 15.5 %collective-permute-start.2 = (f32[128,1024]{1,0:T(8,128)S(1)}, f32[128,1024]{1,0:T(8,128)S(1)}, u32[]{:S(2)}, u32[]{:S(2)}) collective-permute-start(f32[128,1024]{1,0:T(8,128)S(1)} %pad_maximum_fusion), channel_id=1, source_target_pairs={{0,32},{1,225},{2,34},{3,227},{4,36},{5,229},{6,38},{7,231},{8,40}... | collective-permute-start | bytes 1572872 | tf_op jit(solution)/shard_map/ppermute | solution.py:26
  4.7 0.7 collective-permute-start.7
  18.3 12.8 %copy-start.4 = (f32[128,1024]{1,0:T(8,128)}, f32[128,1024]{1,0:T(8,128)S(1)}, u32[]{:S(2)}) copy-start(f32[128,1024]{1,0:T(8,128)S(1)} %collective-permute-done.2.refs_2_) | copy-start | bytes 1572868
  18.3 19.5 %collective-permute-start.3 = (f32[128,1024]{1,0:T(8,128)S(1)}, f32[128,1024]{1,0:T(8,128)}, u32[]{:S(2)}, u32[]{:S(2)}) collective-permute-start(f32[128,1024]{1,0:T(8,128)S(1)} %collective-permute-done.2.refs_2_), channel_id=1, source_target_pairs={{0,16},{1,17},{2,18},{3,19},{4,20},{5,21},{6,22},{7,23},{8,24},{9,... | collective-permute-start | bytes 1572872 | tf_op jit(solution)/shard_map/ppermute | solution.py:26
  19.0 18.7 %collective-permute-start.8 = (f32[128,1024]{1,0:T(8,128)S(1)}, f32[128,1024]{1,0:T(8,128)}, u32[]{:S(2)}, u32[]{:S(2)}) collective-permute-start(f32[128,1024]{1,0:T(8,128)S(1)} %collective-permute-done.2.refs_2_), channel_id=1, source_target_pairs={{0,32},{1,225},{2,34},{3,227},{4,36},{5,229},{6,38},{7,231},{8,40}... | collective-permute-start | bytes 1572872 | tf_op jit(solution)/shard_map/ppermute | solution.py:26
  27.1 10.7 %collective-permute-start.4 = (f32[128,1024]{1,0:T(8,128)S(1)}, f32[128,1024]{1,0:T(8,128)S(1)}, u32[]{:S(2)}, u32[]{:S(2)}) collective-permute-start(f32[128,1024]{1,0:T(8,128)S(1)} %collective-permute-done.2.refs_2_), channel_id=1, source_target_pairs={{0,1},{1,0},{2,3},{3,2},{4,5},{5,4},{6,7},{7,6},{8,9},{9,8},{10,11... | collective-permute-start | bytes 1572872 | tf_op jit(solution)/shard_map/ppermute | solution.py:26
  31.0 23.2 %copy-start.3 = (f32[64,1024]{1,0:T(8,128)S(1)}, f32[64,1024]{1,0:T(8,128)}, u32[]{:S(2)}) copy-start(f32[64,1024]{1,0:T(8,128)} %refs_0_.1) | copy-start | bytes 786436
  31.0 38.0 %all-to-all-start = ((f32[8,64,1024]{2,1,0:T(8,128)}), f32[8,64,1024]{2,1,0:T(8,128)S(1)}, u32[]{:S(2)}, u32[]{:S(2)}) async-start(f32[8,64,1024]{2,1,0:T(8,128)} %broadcast_in_dim.2), calls=%async_computation | async-start | bytes 4194304 | tf_op jit(solution)/shard_map/all_to_all | solution.py:205
  37.8 16.3 %copy-start.5 = (f32[128,1024]{1,0:T(8,128)}, f32[128,1024]{1,0:T(8,128)S(1)}, u32[]{:S(2)}) copy-start(f32[128,1024]{1,0:T(8,128)S(1)} %collective-permute-done.4.refs_4_) | copy-start | bytes 1572868
  37.8 10.8 %collective-permute-start.9 = (f32[128,1024]{1,0:T(8,128)}, f32[128,1024]{1,0:T(8,128)}, u32[]{:S(2)}, u32[]{:S(2)}) collective-permute-start(f32[128,1024]{1,0:T(8,128)} %collective-permute-done.3.refs_3_), channel_id=1, source_target_pairs={{0,32},{1,225},{2,34},{3,227},{4,36},{5,229},{6,38},{7,231},{8,40}... | collective-permute-start | bytes 1572872 | tf_op jit(solution)/shard_map/ppermute | solution.py:26
  38.9 15.2 %collective-permute-start.12 = (f32[128,1024]{1,0:T(8,128)}, f32[128,1024]{1,0:T(8,128)S(1)}, u32[]{:S(2)}, u32[]{:S(2)}) collective-permute-start(f32[128,1024]{1,0:T(8,128)} %collective-permute-done.8.refs_6_), channel_id=1, source_target_pairs={{0,32},{1,225},{2,34},{3,227},{4,36},{5,229},{6,38},{7,231},{8,40}... | collective-permute-start | bytes 1572872 | tf_op jit(solution)/shard_map/ppermute | solution.py:26
  48.5 5.5 %collective-permute-start.11 = (f32[128,1024]{1,0:T(8,128)}, f32[128,1024]{1,0:T(8,128)S(1)}, u32[]{:S(2)}, u32[]{:S(2)}) collective-permute-start(f32[128,1024]{1,0:T(8,128)} %collective-permute-done.9.refs_7_), channel_id=1, source_target_pairs={{0,1},{1,0},{2,3},{3,2},{4,5},{5,4},{6,7},{7,6},{8,9},{9,8},{10,11... | collective-permute-start | bytes 1572872 | tf_op jit(solution)/shard_map/ppermute | solution.py:26
  48.6 7.2 %collective-permute-start.5 = (f32[128,1024]{1,0:T(8,128)}, f32[128,1024]{1,0:T(8,128)S(1)}, u32[]{:S(2)}, u32[]{:S(2)}) collective-permute-start(f32[128,1024]{1,0:T(8,128)} %collective-permute-done.3.refs_3_), channel_id=1, source_target_pairs={{0,1},{1,0},{2,3},{3,2},{4,5},{5,4},{6,7},{7,6},{8,9},{9,8},{10,11... | collective-permute-start | bytes 1572872 | tf_op jit(solution)/shard_map/ppermute | solution.py:26
  49.1 7.5 %collective-permute-start.10 = (f32[128,1024]{1,0:T(8,128)}, f32[128,1024]{1,0:T(8,128)}, u32[]{:S(2)}, u32[]{:S(2)}) collective-permute-start(f32[128,1024]{1,0:T(8,128)} %collective-permute-done.8.refs_6_), channel_id=1, source_target_pairs={{0,1},{1,0},{2,3},{3,2},{4,5},{5,4},{6,7},{7,6},{8,9},{9,8},{10,11... | collective-permute-start | bytes 1572872 | tf_op jit(solution)/shard_map/ppermute | solution.py:26
  54.1 24.3 %copy-start.1 = (f32[128,1024]{1,0:T(8,128)}, f32[128,1024]{1,0:T(8,128)S(1)}, u32[]{:S(2)}) copy-start(f32[128,1024]{1,0:T(8,128)S(1)} %collective-permute-done.12.refs_10_) | copy-start | bytes 1572868
  54.1 14.9 %collective-permute-start.13 = (f32[128,1024]{1,0:T(8,128)}, f32[128,1024]{1,0:T(8,128)S(1)}, u32[]{:S(2)}, u32[]{:S(2)}) collective-permute-start(f32[128,1024]{1,0:T(8,128)} %collective-permute-done.9.refs_7_), channel_id=1, source_target_pairs={{0,32},{1,225},{2,34},{3,227},{4,36},{5,229},{6,38},{7,231},{8,40}... | collective-permute-start | bytes 1572872 | tf_op jit(solution)/shard_map/ppermute | solution.py:26
  54.2 14.1 %collective-permute-start = (f32[64,1024]{1,0:T(8,128)S(1)}, f32[64,1024]{1,0:T(8,128)S(1)}, u32[]{:S(2)}, u32[]{:S(2)}) collective-permute-start(f32[64,1024]{1,0:T(8,128)S(1)} %copy-done.3), channel_id=1, source_target_pairs={{0,16},{1,17},{2,18},{3,19},{4,20},{5,21},{6,22},{7,23},{8,24},{9,... | collective-permute-start | bytes 786440 | tf_op jit(solution)/shard_map/ppermute | solution.py:26
  56.6 12.4 %collective-permute-start.16 = (f32[64,1024]{1,0:T(8,128)S(1)}, f32[64,1024]{1,0:T(8,128)}, u32[]{:S(2)}, u32[]{:S(2)}) collective-permute-start(f32[64,1024]{1,0:T(8,128)S(1)} %slice.6), channel_id=1, source_target_pairs={{0,32},{1,225},{2,34},{3,227},{4,36},{5,229},{6,38},{7,231},{8,40}... | collective-permute-start | bytes 786440 | tf_op jit(solution)/shard_map/ppermute | solution.py:26
  69.0 9.3 %collective-permute-start.18 = (f32[512,1024]{1,0:T(8,128)S(1)}, f32[512,1024]{1,0:T(8,128)}, u32[]{:S(2)}, u32[]{:S(2)}) collective-permute-start(f32[512,1024]{1,0:T(8,128)S(1)} %bitcast.5), channel_id=1, source_target_pairs={{0,1},{1,0},{2,3},{3,2},{4,5},{5,4},{6,7},{7,6},{8,9},{9,8},{10,11... | collective-permute-start | bytes 6291464 | tf_op jit(solution)/shard_map/ppermute | solution.py:26
  69.1 5.0 %collective-permute-start.14 = (f32[128,1024]{1,0:T(8,128)S(1)}, f32[128,1024]{1,0:T(8,128)}, u32[]{:S(2)}, u32[]{:S(2)}) collective-permute-start(f32[128,1024]{1,0:T(8,128)S(1)} %collective-permute-done.12.refs_10_), channel_id=1, source_target_pairs={{0,1},{1,0},{2,3},{3,2},{4,5},{5,4},{6,7},{7,6},{8,9},{9,8},{10,11... | collective-permute-start | bytes 1572872 | tf_op jit(solution)/shard_map/ppermute | solution.py:26
  69.6 8.7 %collective-permute-start.15 = (f32[128,1024]{1,0:T(8,128)S(1)}, f32[128,1024]{1,0:T(8,128)}, u32[]{:S(2)}, u32[]{:S(2)}) collective-permute-start(f32[128,1024]{1,0:T(8,128)S(1)} %collective-permute-done.13.refs_11_), channel_id=1, source_target_pairs={{0,1},{1,0},{2,3},{3,2},{4,5},{5,4},{6,7},{7,6},{8,9},{9,8},{10,11... | collective-permute-start | bytes 1572872 | tf_op jit(solution)/shard_map/ppermute | solution.py:26
  70.6 7.8 %collective-permute-start.17 = (f32[64,1024]{1,0:T(8,128)}, f32[64,1024]{1,0:T(8,128)S(1)}, u32[]{:S(2)}, u32[]{:S(2)}) collective-permute-start(f32[64,1024]{1,0:T(8,128)} %slice.7), channel_id=1, source_target_pairs={{0,32},{1,225},{2,34},{3,227},{4,36},{5,229},{6,38},{7,231},{8,40}... | collective-permute-start | bytes 786440 | tf_op jit(solution)/shard_map/ppermute | solution.py:26
  (6 other events, 22.7 us)
